TPU v7x, 256 devices: a whole 4x4x8 slice. The times are simulated.
256 devices in a mesh: row: 64 (over z, x, y_lo), col: 4 (over y_hi, core).
Axes of the slice: x: 4, y: 4 (y_hi: 2, y_lo: 2; y = y_hi * 2 + y_lo), z: 8, core: 2. Of those that a mesh axis runs over, the one named last changes fastest.
Arguments:
- pair: bfloat16 [1024, 1024, 128], P('row', 'col'), may hold values from -6 to 6
- w_in: bfloat16 [2, 128, 512], replicated, may hold values from -0.5 to 0.5
- w_gate: bfloat16 [2, 128, 128], replicated, may hold values from -0.5 to 0.5
- w_out: bfloat16 [2, 128, 128], replicated, may hold values from -0.5 to 0.5
Outputs:
- pair_out: bfloat16 [1024, 1024, 128], P('row', 'col')
All inputs are finite; a program needn't handle non-finite values.
Results may differ from a plain program's by a relative error of at most 0.018.
Values may be sent and summed in bfloat16 or wider, within the bound.
No kernel may reach another device: no remote copies, remote signals or barrier semaphores. Data moves between devices by JAX's collectives and lax.ppermute only.
A program may use at most 64 MiB of HBM per device.

v0:
```python
import jax
import jax.numpy as jnp
from jax import lax
from jax.sharding import PartitionSpec as P


def layer_norm(value, axis):
    mean = jnp.mean(value, axis=axis, keepdims=True)
    centred = value - mean
    var = jnp.mean(centred * centred, axis=axis, keepdims=True)
    return centred * lax.rsqrt(var + 1e-05)


def outgoing(operands):
    left_slab, right_slab = operands
    partial_sums = jnp.einsum(
        "xcik,xcjk->xcij", left_slab, right_slab, preferred_element_type=jnp.float32
    )
    summed = lax.psum_scatter(
        partial_sums.astype(jnp.bfloat16), "col", scatter_dimension=3, tiled=True
    )
    return summed


def incoming(operands):
    left_slab, right_slab = operands
    return jnp.einsum(
        "xcki,xckj->xcij",
        lax.all_gather(left_slab, "col", axis=3, tiled=True),
        right_slab,
        preferred_element_type=jnp.float32,
    ).astype(jnp.bfloat16)


def regroup(left_values, right_values, contract_fn):
    return contract_fn(
        (
            lax.all_to_all(left_values, "row", split_axis=0, concat_axis=2, tiled=True),
            lax.all_to_all(right_values, "row", split_axis=0, concat_axis=2, tiled=True),
        )
    )


def on_device(pair, w_in, w_gate, w_out):
    hidden = w_out.shape[1]
    groups = lax.axis_size("row")
    share = hidden // groups
    rows_here = pair.shape[0]
    cols_here = pair.shape[1]
    for layer in range(2):
        normed = layer_norm(pair.astype(jnp.float32), -1).astype(jnp.bfloat16)
        proj = jnp.einsum("ijd,de->eij", normed, w_in[layer], preferred_element_type=jnp.float32)
        left_values = (jax.nn.sigmoid(proj[hidden : 2 * hidden]) * proj[:hidden]).astype(
            jnp.bfloat16
        )
        right_values = (jax.nn.sigmoid(proj[3 * hidden :]) * proj[2 * hidden : 3 * hidden]).astype(
            jnp.bfloat16
        )
        left_values = left_values.reshape(groups, share, rows_here, cols_here)
        right_values = right_values.reshape(groups, share, rows_here, cols_here)
        if layer == 0:
            triangle = regroup(left_values, right_values, outgoing)
        else:
            triangle = regroup(left_values, right_values, incoming)
        returned = lax.all_to_all(triangle, "row", split_axis=2, concat_axis=0, tiled=True)
        returned = returned.reshape(hidden, rows_here, cols_here)
        summed = layer_norm(returned.astype(jnp.float32), 0).astype(jnp.bfloat16)
        gate = jax.nn.sigmoid(
            jnp.einsum("ijd,de->ije", normed, w_gate[layer], preferred_element_type=jnp.float32)
        )
        update = gate * jnp.einsum(
            "hij,hd->ijd", summed, w_out[layer], preferred_element_type=jnp.float32
        )
        pair = (pair.astype(jnp.float32) + update).astype(jnp.bfloat16)
    return pair


def solution(mesh):
    placed = (P("row", "col", None), P(), P(), P())
    return jax.shard_map(
        on_device, mesh=mesh, in_specs=placed, out_specs=P("row", "col", None), check_vma=False
    )
```

profile of v0, /device:TPU:1, one launch (start us, length us, event | category | flops | bytes accessed | tf_op | source)
XLA Modules:
  0.0 334.9 jit_solution(1628852740009880137)
XLA Ops:
  6.5 1.5 copy.66
  11.0 1.7 copy.72
  12.7 13.5 %all-to-all-start.1 = ((bf16[64,2,16,256]{3,2,1,0:T(8,128)(2,1)}), bf16[64,2,16,256]{3,2,1,0:T(8,128)(2,1)S(1)}, u32[]{:S(2)}, u32[]{:S(2)}) async-start(bf16[64,2,16,256]{3,2,1,0:T(8,128)(2,1)} %bitcast.111), calls=%async_computation.1 | async-start | bytes 2097152 | tf_op jit(solution)/shard_map/all_to_all | solution.py:39
  26.2 1.7 copy.70
  27.9 24.4 %all-to-all-done.1 = bf16[64,2,16,256]{3,2,1,0:T(8,128)(2,1)S(1)} async-done(((bf16[64,2,16,256]{3,2,1,0:T(8,128)(2,1)}), bf16[64,2,16,256]{3,2,1,0:T(8,128)(2,1)S(1)}, u32[]{:S(2)}, u32[]{:S(2)}) %all-to-all-start.1) | async-done | bytes 1048608 | tf_op jit(solution)/shard_map/all_to_all | solution.py:39
  52.3 8.0 %all-to-all-start = ((bf16[64,2,16,256]{3,2,1,0:T(8,128)(2,1)}), bf16[64,2,16,256]{3,2,1,0:T(8,128)(2,1)S(1)}, u32[]{:S(2)}, u32[]{:S(2)}) async-start(bf16[64,2,16,256]{3,2,1,0:T(8,128)(2,1)} %bitcast.109), calls=%async_computation | async-start | bytes 2097152 | tf_op jit(solution)/shard_map/all_to_all | solution.py:38
  61.4 24.7 %all-to-all-done = bf16[64,2,16,256]{3,2,1,0:T(8,128)(2,1)S(1)} async-done(((bf16[64,2,16,256]{3,2,1,0:T(8,128)(2,1)}), bf16[64,2,16,256]{3,2,1,0:T(8,128)(2,1)S(1)}, u32[]{:S(2)}, u32[]{:S(2)}) %all-to-all-start) | async-done | bytes 1048608 | tf_op jit(solution)/shard_map/all_to_all | solution.py:38
  86.2 3.2 convert_bitcast_fusion
  89.4 56.7 %reduce-scatter.2.cloned.1.call-done = bf16[1,2,1024,256]{3,2,1,0:T(8,128)(2,1)} async-done(((bf16[1,2,1024,1024]{3,2,1,0:T(8,128)(2,1)}), bf16[1,2,1024,256]{3,2,1,0:T(8,128)(2,1)}) %reduce-scatter.2.cloned.1.call-update) | async-done | bytes 1048592 | tf_op jit(solution)/shard_map/reduce_scatter | solution.py:19
  146.1 3.3 copy.74
  149.4 10.2 %all-to-all-start.2 = ((bf16[1,2,1024,256]{3,1,0,2:T(2,128)(2,1)}), bf16[1,2,1024,256]{3,1,0,2:T(2,128)(2,1)S(1)}, u32[]{:S(2)}, u32[]{:S(2)}) async-start(bf16[1,2,1024,256]{3,1,0,2:T(2,128)(2,1)} %copy.74), calls=%async_computation.3 | async-start | bytes 2097152 | tf_op jit(solution)/shard_map/all_to_all | solution.py:65
  159.8 1.8 fusion.48
  161.6 24.0 %all-to-all-done.2 = bf16[1,2,1024,256]{3,1,0,2:T(2,128)(2,1)S(1)} async-done(((bf16[1,2,1024,256]{3,1,0,2:T(2,128)(2,1)}), bf16[1,2,1024,256]{3,1,0,2:T(2,128)(2,1)S(1)}, u32[]{:S(2)}, u32[]{:S(2)}) %all-to-all-start.2) | async-done | bytes 1048608 | tf_op jit(solution)/shard_map/all_to_all | solution.py:65
  186.6 1.4 fusion.38
  190.8 2.4 convert_reduce_fusion
  196.0 1.7 copy.80
  197.6 33.8 %all_to_all.81 = bf16[64,2,16,256]{3,2,1,0:T(8,128)(2,1)S(1)} all-to-all(bf16[64,2,16,256]{3,2,1,0:T(8,128)(2,1)} %bitcast.112), channel_id=1, replica_groups=mesh['row'=64,'col'=4] {'row'}, dimensions={0} | all-to-all | bytes 2097152 | tf_op jit(solution)/shard_map/all_to_all | solution.py:38
  233.8 33.0 %all_to_all.82 = bf16[64,2,16,256]{3,2,1,0:T(8,128)(2,1)S(1)} all-to-all(bf16[64,2,16,256]{3,2,1,0:T(8,128)(2,1)S(1)} %bitcast.115), channel_id=1, replica_groups=mesh['row'=64,'col'=4] {'row'}, dimensions={0} | all-to-all | bytes 2097152 | tf_op jit(solution)/shard_map/all_to_all | solution.py:39
  266.9 15.6 %all-gather.2.cloned.1.call-done = bf16[1,2,1024,1024]{2,3,1,0:T(8,128)(2,1)} async-done(((bf16[1,2,1024,256]{2,3,1,0:T(8,128)(2,1)}), bf16[1,2,1024,1024]{2,3,1,0:T(8,128)(2,1)}) %all-gather.2.cloned.1.call-update) | async-done | bytes 4194320 | tf_op jit(solution)/shard_map/all_gather | solution.py:29
  282.5 3.4 %fusion.43 = bf16[1,2,1024,256]{3,2,1,0:T(8,128)(2,1)S(1)} fusion(bf16[2,1024,256]{2,1,0:T(8,128)(2,1)S(1)} %bitcast.119, bf16[1,2,1024,1024]{2,3,1,0:T(8,128)(2,1)} %all-gather.2.cloned.1.call-done), kind=kOutput, calls=%fused_computation.60 | convolution fusion | flops 1074266112 | bytes 6291456 | tf_op jit(solution)/shard_map/xcki,xckj->xcij/dot_general | solution.py:27
  285.9 2.0 copy.85
  288.0 8.7 %all-to-all-start.5 = ((bf16[1,2,1024,256]{3,1,0,2:T(2,128)(2,1)}), bf16[1,2,1024,256]{3,1,0,2:T(2,128)(2,1)S(1)}, u32[]{:S(2)}, u32[]{:S(2)}) async-start(bf16[1,2,1024,256]{3,1,0,2:T(2,128)(2,1)} %copy.85), calls=%async_computation.6 | async-start | bytes 2097152 | tf_op jit(solution)/shard_map/all_to_all | solution.py:65
  296.7 1.8 fusion.51
  298.6 24.9 %all-to-all-done.5 = bf16[1,2,1024,256]{3,1,0,2:T(2,128)(2,1)S(1)} async-done(((bf16[1,2,1024,256]{3,1,0,2:T(2,128)(2,1)}), bf16[1,2,1024,256]{3,1,0,2:T(2,128)(2,1)S(1)}, u32[]{:S(2)}, u32[]{:S(2)}) %all-to-all-start.5) | async-done | bytes 1048608 | tf_op jit(solution)/shard_map/all_to_all | solution.py:65
  (46 shorter events, 17.6 us)
Async XLA Ops:
  6.5 2.0 copy-start.2
  12.7 39.6 %all-to-all-start.1 = ((bf16[64,2,16,256]{3,2,1,0:T(8,128)(2,1)}), bf16[64,2,16,256]{3,2,1,0:T(8,128)(2,1)S(1)}, u32[]{:S(2)}, u32[]{:S(2)}) async-start(bf16[64,2,16,256]{3,2,1,0:T(8,128)(2,1)} %bitcast.111), calls=%async_computation.1 | async-start | bytes 2097152 | tf_op jit(solution)/shard_map/all_to_all | solution.py:39
  52.3 33.8 %all-to-all-start = ((bf16[64,2,16,256]{3,2,1,0:T(8,128)(2,1)}), bf16[64,2,16,256]{3,2,1,0:T(8,128)(2,1)S(1)}, u32[]{:S(2)}, u32[]{:S(2)}) async-start(bf16[64,2,16,256]{3,2,1,0:T(8,128)(2,1)} %bitcast.109), calls=%async_computation | async-start | bytes 2097152 | tf_op jit(solution)/shard_map/all_to_all | solution.py:38
  60.3 85.8 %reduce-scatter.2.cloned.1.call-start = ((), (), s32[]{:S(2)}) async-start(), calls=%async_computation.7 | async-start | bytes 5242880 | tf_op jit(solution)/shard_map/reduce_scatter | solution.py:19
  61.4 24.8 %copy-start = (bf16[1,2,64,16,256]{4,3,2,1,0:T(8,128)(2,1)S(1)}, bf16[1,2,64,16,256]{4,3,2,1,0:T(8,128)(2,1)}, u32[]{:S(2)}) copy-start(bf16[1,2,64,16,256]{4,3,2,1,0:T(8,128)(2,1)} %copy.73) | copy-start | bytes 3145732
  89.4 70.4 %copy-start.3 = (bf16[2,128,128]{2,1,0:T(8,128)(2,1)S(1)}, bf16[2,128,128]{2,1,0:T(8,128)(2,1)}, u32[]{:S(2)}) copy-start(bf16[2,128,128]{2,1,0:T(8,128)(2,1)} %param.6) | copy-start | bytes 196612
  149.4 36.3 %all-to-all-start.2 = ((bf16[1,2,1024,256]{3,1,0,2:T(2,128)(2,1)}), bf16[1,2,1024,256]{3,1,0,2:T(2,128)(2,1)S(1)}, u32[]{:S(2)}, u32[]{:S(2)}) async-start(bf16[1,2,1024,256]{3,1,0,2:T(2,128)(2,1)} %copy.74), calls=%async_computation.3 | async-start | bytes 2097152 | tf_op jit(solution)/shard_map/all_to_all | solution.py:65
  159.6 122.9 %all-gather.2.cloned.1.call-start = ((), (), s32[]{:S(2)}) async-start(), calls=%async_computation.8 | async-start | bytes 5242880 | tf_op jit(solution)/shard_map/all_gather | solution.py:29
  288.0 35.5 %all-to-all-start.5 = ((bf16[1,2,1024,256]{3,1,0,2:T(2,128)(2,1)}), bf16[1,2,1024,256]{3,1,0,2:T(2,128)(2,1)S(1)}, u32[]{:S(2)}, u32[]{:S(2)}) async-start(bf16[1,2,1024,256]{3,1,0,2:T(2,128)(2,1)} %copy.85), calls=%async_computation.6 | async-start | bytes 2097152 | tf_op jit(solution)/shard_map/all_to_all | solution.py:65
  324.1 1.6 copy-start.1
  324.2 1.6 copy-start.4
Sparse Core Ops, SparseCore 0:
  89.5 56.5 reduce-scatter.1
  233.0 49.4 all-gather.1
where the time goes:
time: 337 us; the launch traced here: 335 us
  waiting for transfers between devices  170 us (50%)
  blocking collectives  66.8 us (20%)
  starting transfers between devices  40.6 us (12%)
  local copies, waits for them, and re-layouts  19.6 us (6%)
  matrix products  16.3 us (5%)
  between operations  13.7 us (4%)
  other arithmetic  7.47 us (2%)
    reduce_scatter x1, waiting for transfers between devices, outgoing(): lax.psum_scatter(partial_sums.astype(jnp.bfloat16), 'col', scatter_dimens...  56.7 us
    all_to_all x2, waiting for transfers between devices, on_device(): lax.all_to_all(triangle, 'row', split_axis=2, concat_axis=0, tiled=True)  48.9 us
    all_to_all x1, blocking collectives, regroup(): lax.all_to_all(left_values, 'row', split_axis=0, concat_axis=2, tiled=True)  33.8 us
    all_to_all x1, blocking collectives, regroup(): lax.all_to_all(right_values, 'row', split_axis=0, concat_axis=2, tiled=True)  33 us
    all_to_all x1, waiting for transfers between devices, regroup(): lax.all_to_all(left_values, 'row', split_axis=0, concat_axis=2, tiled=True)  24.7 us
    all_to_all x1, waiting for transfers between devices, regroup(): lax.all_to_all(right_values, 'row', split_axis=0, concat_axis=2, tiled=True)  24.4 us
    all_to_all x2, starting transfers between devices, on_device(): lax.all_to_all(triangle, 'row', split_axis=2, concat_axis=0, tiled=True)  18.9 us
    all_gather x1, waiting for transfers between devices, incoming(): lax.all_gather(left_slab, 'col', axis=3, tiled=True)  15.6 us
  transfers between devices with their start and end apart: 6, of which 6 were waited for; matrix products, arithmetic and copies ran while one was open for 2% of the time, Pallas kernels for 0%

commit v1 on v0

v1 whole, which is shorter than its diff:
```python
import functools

import jax
import jax.numpy as jnp
from jax import lax
from jax.experimental import pallas as pl
from jax.experimental.pallas import tpu as pltpu
from jax.sharding import Mesh, PartitionSpec as P

AXES = ("z", "x", "yl", "yh", "core")
CHIPS = ("z", "x", "yl", "yh")
F32, BF16 = jnp.float32, jnp.bfloat16
VMEM = pl.BlockSpec(memory_space=pltpu.VMEM)
SMEM = pl.BlockSpec(memory_space=pltpu.SMEM)


def params():
    return pltpu.CompilerParams(vmem_limit_bytes=48 * 1024 * 1024)


def sigmoid(v):
    return 0.5 * jnp.tanh(0.5 * v) + 0.5


def norm(v):
    mean = jnp.mean(v, axis=0, keepdims=True)
    centred = v - mean
    var = jnp.mean(centred * centred, axis=0, keepdims=True)
    return centred * lax.rsqrt(var + 1e-05)


def turned(w):
    return w.astype(F32).T.astype(BF16)


def dot(a, b):
    return jnp.dot(a, b, preferred_element_type=F32)


def project(x, w_t, r, rows, wide, hidden):
    proj = dot(w_t, x)
    left = sigmoid(proj[hidden : 2 * hidden]) * proj[:hidden]
    right = sigmoid(proj[3 * hidden :]) * proj[2 * hidden : 3 * hidden]
    for half in range(wide.shape[0]):
        cols = slice(half * 128, half * 128 + 128)
        wide[half, pl.ds(r, hidden, stride=2 * rows), :] = left[:, cols]
        wide[half, pl.ds(rows + r, hidden, stride=2 * rows), :] = right[:, cols]


def pack(wide, out_ref):
    hidden, depth, _ = out_ref.shape

    def step(c, _):
        for half in range(wide.shape[0]):
            rows = wide[half, pl.ds(pl.multiple_of(c * 8 * depth, 8 * depth), 8 * depth), :]
            out_ref[pl.ds(c * 8, 8), :, half * 128 : half * 128 + 128] = rows.reshape(
                8, depth, 128
            ).astype(BF16)
        return 0

    lax.fori_loop(0, hidden // 8, step, 0)


def first_kernel(pair_ref, w_in_ref, out_ref, wide, w_t):
    rows, _, hidden = pair_ref.shape
    w_t[...] = turned(w_in_ref[...])

    def step(r, _):
        x = norm(pair_ref[r].astype(F32).T).astype(BF16)
        project(x, w_t[...], r, rows, wide, hidden)
        return 0

    lax.fori_loop(0, rows, step, 0, unroll=2)
    pack(wide, out_ref)


def first(pair, w_in):
    rows, cols, hidden = pair.shape
    return pl.pallas_call(
        first_kernel,
        out_shape=jax.ShapeDtypeStruct((hidden, 2 * rows, cols), BF16),
        in_specs=[VMEM, VMEM],
        out_specs=VMEM,
        scratch_shapes=[
            pltpu.VMEM((cols // 128, hidden * 2 * rows, 128), F32),
            pltpu.VMEM((w_in.shape[1], hidden), BF16),
        ],
        compiler_params=params(),
        name="first",
    )(pair, w_in)


def gate_kernel(pair_ref, w_gate_ref, z_ref, gate_ref, w_t):
    rows = pair_ref.shape[0]
    w_t[...] = turned(w_gate_ref[...])

    def step(r, _):
        z = pair_ref[r].astype(F32).T
        x = norm(z).astype(BF16)
        z_ref[r] = z.astype(BF16)
        gate_ref[r] = sigmoid(dot(w_t[...], x))
        return 0

    lax.fori_loop(0, rows, step, 0, unroll=2)


def gate(pair, w_gate):
    rows, cols, hidden = pair.shape
    return pl.pallas_call(
        gate_kernel,
        out_shape=(
            jax.ShapeDtypeStruct((rows, hidden, cols), BF16),
            jax.ShapeDtypeStruct((rows, hidden, cols), F32),
        ),
        in_specs=[VMEM, VMEM],
        out_specs=(VMEM, VMEM),
        scratch_shapes=[pltpu.VMEM((hidden, hidden), BF16)],
        compiler_params=params(),
        name="gate",
    )(pair, w_gate)


def gate_turned_kernel(z_ref, w_gate_ref, gate_ref, w_t):
    w_t[...] = turned(w_gate_ref[...])

    def step(r, _):
        x = norm(z_ref[r].astype(F32)).astype(BF16)
        gate_ref[r] = sigmoid(dot(w_t[...], x))
        return 0

    lax.fori_loop(0, z_ref.shape[0], step, 0, unroll=2)


def gate_turned(z, w_gate):
    rows, hidden, cols = z.shape
    return pl.pallas_call(
        gate_turned_kernel,
        out_shape=jax.ShapeDtypeStruct((rows, hidden, cols), F32),
        in_specs=[VMEM, VMEM],
        out_specs=VMEM,
        scratch_shapes=[pltpu.VMEM((hidden, hidden), BF16)],
        compiler_params=params(),
        name="gate_turned",
    )(z, w_gate)


def outgoing_kernel(add, which_ref, got_ref, *refs):
    out_ref = refs[-1]
    blocks, _, depth, cols = got_ref.shape
    rows = depth // 2
    per = cols // rows
    for yo in range(2):
        at = (yo * 2 + which_ref[0]) * per
        total = None
        for yk in range(2):
            a = got_ref[:, yk, :rows, :].reshape(blocks * rows, cols)
            b = got_ref[pl.ds(at, per), yk, rows:, :].reshape(cols, cols)
            part = lax.dot_general(a, b, (((1,), (1,)), ((), ())), preferred_element_type=F32)
            total = part if total is None else total + part
        total = total.reshape(blocks, rows, cols)
        if add:
            total = total + refs[0][:, yo].astype(F32)
        out_ref[:, yo] = total.astype(BF16)


def outgoing(got, core):
    src, depth, cols = got.shape
    got = got.reshape(src // 2, 2, depth, cols)
    shape = jax.ShapeDtypeStruct((src // 2, 2, depth // 2, cols), BF16)

    def call(add, which, *more):
        return pl.pallas_call(
            functools.partial(outgoing_kernel, add),
            out_shape=shape,
            in_specs=[SMEM, VMEM] + [VMEM] * len(more),
            out_specs=VMEM,
            compiler_params=params(),
            name="outgoing",
        )(which, got, *more)

    other = call(False, (1 - core).reshape(1))
    other = lax.ppermute(other, "core", [(0, 1), (1, 0)])
    return call(True, core.reshape(1), other).reshape(src, depth // 2, cols)


def incoming_kernel(which_ref, got_ref, left_ref, out_ref):
    blocks, _, depth, cols = got_ref.shape
    rows = depth // 2
    per = cols // rows
    for own in (True, False):
        core = which_ref[0] if own else 1 - which_ref[0]
        for yi in range(2):
            left = got_ref[:, yi, :rows, :] if own else left_ref[:, yi]
            left = left.reshape(blocks * rows, cols)
            at = (yi * 2 + core) * per
            for yo in range(2):
                right = got_ref[:, yo, rows:, :].reshape(blocks * rows, cols)
                part = lax.dot_general(
                    left, right, (((0,), (0,)), ((), ())), preferred_element_type=F32
                )
                out_ref[pl.ds(at, per), yo] = part.reshape(per, rows, cols).astype(BF16)


def incoming(got, core):
    src, depth, cols = got.shape
    got = got.reshape(src // 2, 2, depth, cols)
    left = lax.ppermute(got[:, :, : depth // 2], "core", [(0, 1), (1, 0)])
    out = pl.pallas_call(
        incoming_kernel,
        out_shape=jax.ShapeDtypeStruct((src // 2, 2, depth // 2, cols), BF16),
        in_specs=[SMEM, VMEM, VMEM],
        out_specs=VMEM,
        compiler_params=params(),
        name="incoming",
    )(core.reshape(1), got, left)
    return out.reshape(src, depth // 2, cols)


def normed_rows(tri_ref, flat):
    hidden, rows, cols = tri_ref.shape
    for half in range(cols // 128):
        lanes = slice(half * 128, half * 128 + 128)
        zero = jnp.zeros((rows, 128), F32)

        def add(c, total):
            return total + tri_ref[c, :, lanes].astype(F32)

        mean = lax.fori_loop(0, hidden, add, zero, unroll=8) * (1.0 / hidden)

        def square(c, total):
            centred = tri_ref[c, :, lanes].astype(F32) - mean
            return total + centred * centred

        var = lax.fori_loop(0, hidden, square, zero, unroll=8) * (1.0 / hidden)
        scale = lax.rsqrt(var + 1e-05)

        def write(c, _):
            flat[half, pl.ds(pl.multiple_of(c * rows, rows), rows), :] = (
                tri_ref[c, :, lanes].astype(F32) - mean
            ) * scale
            return 0

        lax.fori_loop(0, hidden, write, 0, unroll=8)


def row_of(flat, r, hidden, rows):
    return jnp.concatenate(
        [flat[half, pl.ds(r, hidden, stride=rows), :] for half in range(flat.shape[0])], axis=1
    ).astype(BF16)


def middle_kernel(tri_ref, z_ref, gate_ref, w_out_ref, w_in_ref, out_ref, z_new_ref, flat, wide, w_out_t, w_in_t):
    hidden, rows, _ = tri_ref.shape
    w_out_t[...] = turned(w_out_ref[...])
    w_in_t[...] = turned(w_in_ref[...])
    normed_rows(tri_ref, flat)

    def step(r, _):
        update = gate_ref[r] * dot(w_out_t[...], row_of(flat, r, hidden, rows))
        z = (z_ref[r].astype(F32) + update).astype(BF16)
        z_new_ref[r] = z
        x = norm(z.astype(F32)).astype(BF16)
        project(x, w_in_t[...], r, rows, wide, hidden)
        return 0

    lax.fori_loop(0, rows, step, 0, unroll=2)
    pack(wide, out_ref)


def middle(tri, z, gates, w_out, w_in):
    hidden, rows, cols = tri.shape
    return pl.pallas_call(
        middle_kernel,
        out_shape=(
            jax.ShapeDtypeStruct((hidden, 2 * rows, cols), BF16),
            jax.ShapeDtypeStruct((rows, hidden, cols), BF16),
        ),
        in_specs=[VMEM] * 5,
        out_specs=(VMEM, VMEM),
        scratch_shapes=[
            pltpu.VMEM((cols // 128, hidden * rows, 128), F32),
            pltpu.VMEM((cols // 128, hidden * 2 * rows, 128), F32),
            pltpu.VMEM((hidden, hidden), BF16),
            pltpu.VMEM((w_in.shape[1], hidden), BF16),
        ],
        compiler_params=params(),
        name="middle",
    )(tri, z, gates, w_out, w_in)


def last_kernel(tri_ref, z_ref, gate_ref, w_out_ref, out_ref, flat, w_out_t):
    hidden, rows, _ = tri_ref.shape
    w_out_t[...] = turned(w_out_ref[...])
    normed_rows(tri_ref, flat)

    def step(r, _):
        update = gate_ref[r] * dot(w_out_t[...], row_of(flat, r, hidden, rows))
        out_ref[r] = (z_ref[r].astype(F32) + update).T.astype(BF16)
        return 0

    lax.fori_loop(0, rows, step, 0, unroll=2)


def last(tri, z, gates, w_out):
    hidden, rows, cols = tri.shape
    return pl.pallas_call(
        last_kernel,
        out_shape=jax.ShapeDtypeStruct((rows, cols, hidden), BF16),
        in_specs=[VMEM] * 4,
        out_specs=VMEM,
        scratch_shapes=[
            pltpu.VMEM((cols // 128, hidden * rows, 128), F32),
            pltpu.VMEM((hidden, hidden), BF16),
        ],
        compiler_params=params(),
        name="last",
    )(tri, z, gates, w_out)


def exchange(blocks):
    return lax.all_to_all(blocks, CHIPS, split_axis=0, concat_axis=0, tiled=True)


def on_device(pair, w_in, w_gate, w_out):
    core = lax.axis_index("core")
    z, gates = gate(pair, w_gate[0])
    got = exchange(first(pair, w_in[0]))
    tri = exchange(outgoing(got, core))
    sent, z = middle(tri, z, gates, w_out[0], w_in[1])
    gates = gate_turned(z, w_gate[1])
    got = exchange(sent)
    tri = exchange(incoming(got, core))
    return last(tri, z, gates, w_out[1])


def solution(mesh):
    mesh = Mesh(mesh.devices.reshape(8, 4, 2, 2, 2), AXES)
    placed = P(("z", "x", "yl"), ("yh", "core"), None)
    return jax.shard_map(
        on_device, mesh=mesh, in_specs=(placed, P(), P(), P()), out_specs=placed, check_vma=False
    )
```

time: 337 us -> 241 us (0.72)
  waiting for transfers between devices: 170 us -> 100 us
  Pallas kernels: 0 us -> 33.5 us
  matrix products: 16.3 us -> 0 us
  between operations: 13.7 us -> 0.14 us
  local copies, waits for them, and re-layouts: 19.6 us -> 7.22 us
  blocking collectives: 66.8 us -> 55.9 us
  other arithmetic: 7.47 us -> 0 us
    reduce_scatter x1 -> x0, waiting for transfers between devices: 56.7 us -> none  [outgoing(): lax.psum_scatter(partial_sums.astype(jnp.bfloat16), 'col', scatter_dimens...]
    pallas_call x0 -> x8, Pallas kernels: none -> 33.5 us  [the longest x1 10.9 us: middle(): pl.pallas_call(middle_kernel, out_shape=(jax.ShapeDtypeStruct((hidden, 2...]
    dot_general x8 -> x0, matrix products: 16.3 us -> none  [the longest x2 3.67 us: on_device(): jnp.einsum('ijd,de->ije', normed, w_gate[layer], preferred_element_type=j...]
    all_gather x1 -> x0, waiting for transfers between devices: 15.6 us -> none  [incoming(): lax.all_gather(left_slab, 'col', axis=3, tiled=True)]
    all_to_all x2 -> x1, blocking collectives: 66.8 us -> 55.9 us  [exchange(): lax.all_to_all(blocks, CHIPS, split_axis=0, concat_axis=0, tiled=True)]
    convert_element_type x9 -> x0, local copies, waits for them, and re-layouts: 10.9 us -> none  [the longest x2 3.36 us: on_device(): (jax.nn.sigmoid(proj[hidden:2 * hidden]) * proj[:hidden]).astype(jnp.bflo...]
    ppermute x0 -> x2, starting transfers between devices: none -> 9.24 us  [the longest x1 5.12 us: incoming(): left = lax.ppermute(got[:, :, :depth // 2], 'core', [(0, 1), (1, 0)])]
    all_to_all x4 -> x3, starting transfers between devices: 40.4 us -> 33.3 us  [exchange(): lax.all_to_all(blocks, CHIPS, split_axis=0, concat_axis=0, tiled=True)]
  transfers between devices with their start and end apart: 6 -> 5, of which waited for: 6 -> 5; matrix products, arithmetic and copies ran while one was open for 2% -> 0% of each run, Pallas kernels for 0% -> 2%
where the time goes in v1:
time: 241 us; the launch traced here: 239 us
  waiting for transfers between devices  100 us (41%)
  blocking collectives  55.9 us (23%)
  starting transfers between devices  42.5 us (18%)
  Pallas kernels  33.5 us (14%)
  local copies, waits for them, and re-layouts  7.22 us (3%)
    all_to_all x3, waiting for transfers between devices, exchange(): lax.all_to_all(blocks, CHIPS, split_axis=0, concat_axis=0, tiled=True)  95.5 us
    all_to_all x1, blocking collectives, exchange(): lax.all_to_all(blocks, CHIPS, split_axis=0, concat_axis=0, tiled=True)  55.9 us
    all_to_all x3, starting transfers between devices, exchange(): lax.all_to_all(blocks, CHIPS, split_axis=0, concat_axis=0, tiled=True)  33.3 us
    pallas_call x1, Pallas kernels, middle(): pl.pallas_call(middle_kernel, out_shape=(jax.ShapeDtypeStruct((hidden, 2...  10.9 us
    pallas_call x1, Pallas kernels, first(): pl.pallas_call(first_kernel, out_shape=jax.ShapeDtypeStruct((hidden, 2 *...  6.97 us
    unnamed x16, local copies, waits for them, and re-layouts  6.1 us
    pallas_call x1, Pallas kernels, last(): pl.pallas_call(last_kernel, out_shape=jax.ShapeDtypeStruct((rows, cols, h...  5.84 us
    ppermute x1, starting transfers between devices, incoming(): left = lax.ppermute(got[:, :, :depth // 2], 'core', [(0, 1), (1, 0)])  5.12 us
  transfers between devices with their start and end apart: 5, of which 5 were waited for; matrix products, arithmetic and copies ran while one was open for 0% of the time, Pallas kernels for 2%

profile of v1, /device:TPU:1, one launch (start us, length us, event | category | flops | bytes accessed | tf_op | source)
XLA Modules:
  0.0 239.3 jit_solution(7105793888565855322)
XLA Ops:
  0.0 1.0 slice_bitcast_fusion
  1.0 1.2 copy-done.1
  2.2 7.0 %first.1 = bf16[128,32,256]{2,1,0:T(8,128)(2,1)S(1)} custom-call(bf16[16,256,128]{2,1,0:T(8,128)(2,1)S(1)} %copy-done.1, bf16[128,512]{1,0:T(8,128)(2,1)S(1)} %get-tuple-element.14.w_in_ref), custom_call_target="tpu_custom_call" | custom-call | tf_op jit(solution)/shard_map/first/pallas_call | solution.py:79
  9.2 1.3 copy-done
  10.5 16.3 %all-to-all-start = ((bf16[128,32,256]{2,1,0:T(8,128)(2,1)}), bf16[128,32,256]{2,1,0:T(8,128)(2,1)S(1)}, u32[]{:S(2)}, u32[]{:S(2)}) async-start(bf16[128,32,256]{2,1,0:T(8,128)(2,1)} %copy-done), calls=%async_computation | async-start | bytes 4194304 | tf_op jit(solution)/shard_map/all_to_all | solution.py:321
  26.9 48.2 %all-to-all-done = bf16[128,32,256]{2,1,0:T(8,128)(2,1)S(1)} async-done(((bf16[128,32,256]{2,1,0:T(8,128)(2,1)}), bf16[128,32,256]{2,1,0:T(8,128)(2,1)S(1)}, u32[]{:S(2)}, u32[]{:S(2)}) %all-to-all-start) | async-done | bytes 2097184 | tf_op jit(solution)/shard_map/all_to_all | solution.py:321
  75.8 4.1 %collective-permute-start = (bf16[64,2,16,256]{3,2,1,0:T(8,128)(2,1)S(1)}, bf16[64,2,16,256]{3,2,1,0:T(8,128)(2,1)S(1)}, u32[]{:S(2)}, u32[]{:S(2)}) collective-permute-start(bf16[64,2,16,256]{3,2,1,0:T(8,128)(2,1)S(1)} %outgoing.2), channel_id=1, source_target_pairs={{0,1},{1,0},{2,3},{3,2},{4,5},{5,4},{6,7},{7,6},{8,9},{9,8},{10,11... | collective-permute-start | bytes 3145736 | tf_op jit(solution)/shard_map/ppermute | solution.py:182
  79.9 2.3 collective-permute-done.refs_0_
  82.2 1.7 outgoing.3
  84.0 8.2 %all-to-all-start.1 = ((bf16[128,16,256]{2,1,0:T(8,128)(2,1)}), bf16[128,16,256]{2,1,0:T(8,128)(2,1)S(1)}, u32[]{:S(2)}, u32[]{:S(2)}) async-start(bf16[128,16,256]{2,1,0:T(8,128)(2,1)} %bitcast.4), calls=%async_computation.1 | async-start | bytes 2097152 | tf_op jit(solution)/shard_map/all_to_all | solution.py:321
  92.2 2.9 %gate.1 = (bf16[16,128,256]{2,1,0:T(8,128)(2,1)S(1)}, f32[16,128,256]{2,1,0:T(8,128)S(1)}) custom-call(bf16[16,256,128]{2,1,0:T(8,128)(2,1)S(1)} %copy-done.2, bf16[128,128]{1,0:T(8,128)(2,1)S(1)} %get-tuple-element.18.w_gate_ref), custom_call_target="tpu_custom_call" | custom-call | tf_op jit(solution)/shard_map/gate/pallas_call | solution.py:109
  95.1 1.3 copy-done.3
  96.4 1.0 copy-done.4
  97.4 22.4 %all-to-all-done.1.tri_ref = bf16[128,16,256]{2,1,0:T(8,128)(2,1)S(1)} async-done(((bf16[128,16,256]{2,1,0:T(8,128)(2,1)}), bf16[128,16,256]{2,1,0:T(8,128)(2,1)S(1)}, u32[]{:S(2)}, u32[]{:S(2)}) %all-to-all-start.1) | async-done | bytes 1048608 | tf_op jit(solution)/shard_map/all_to_all | solution.py:321
  119.8 1.2 copy-done.5
  121.0 10.9 %middle.1 = (bf16[128,32,256]{2,1,0:T(8,128)(2,1)S(1)}, bf16[16,128,256]{2,1,0:T(8,128)(2,1)S(1)}) custom-call(bf16[128,16,256]{2,1,0:T(8,128)(2,1)S(1)} %all-to-all-done.1.tri_ref, bf16[16,128,256]{2,1,0:T(8,128)(2,1)S(1)} %copy-done.5, f32[16,128,256]{2,1,0:T(8,128)} %copy-done.3, bf16[128,128]{1,0:T(8,128)(2,1)S(1)} %get-tuple-element.16.w_out_ref, ...), custom_call_target="tpu_custom_call" | custom-call | tf_op jit(solution)/shard_map/middle/pallas_call | solution.py:272
  131.9 55.9 %all_to_all.20 = bf16[128,32,256]{2,1,0:T(8,128)(2,1)S(1)} all-to-all(bf16[128,32,256]{2,1,0:T(8,128)(2,1)S(1)} %get-tuple-element.11), channel_id=1, replica_groups=mesh['z'=8,'x'=4,'yl'=2,'yh'=2,'core'=2] {'z','x','yl','yh'}, dimensions={0} | all-to-all | bytes 4194304 | tf_op jit(solution)/shard_map/all_to_all | solution.py:321
  187.9 5.1 %collective-permute-start.1 = (bf16[64,2,16,256]{3,2,1,0:T(8,128)(2,1)S(1)}, bf16[64,2,16,256]{3,2,1,0:T(8,128)(2,1)S(1)}, u32[]{:S(2)}, u32[]{:S(2)}) collective-permute-start(bf16[64,2,16,256]{3,2,1,0:T(8,128)(2,1)S(1)} %slice.28), channel_id=1, source_target_pairs={{0,1},{1,0},{2,3},{3,2},{4,5},{5,4},{6,7},{7,6},{8,9},{9,8},{10,11... | collective-permute-start | bytes 3145736 | tf_op jit(solution)/shard_map/ppermute | solution.py:207
  193.0 2.3 collective-permute-done.1.left_ref
  195.3 2.2 incoming.1
  197.5 8.7 %all-to-all-start.3 = ((bf16[128,16,256]{2,1,0:T(8,128)(2,1)}), bf16[128,16,256]{2,1,0:T(8,128)(2,1)}, u32[]{:S(2)}, u32[]{:S(2)}) async-start(bf16[128,16,256]{2,1,0:T(8,128)(2,1)} %bitcast.9), calls=%async_computation.3 | async-start | bytes 2097152 | tf_op jit(solution)/shard_map/all_to_all | solution.py:321
  206.3 2.2 gate_turned.1.gate_ref
  208.5 24.9 %all-to-all-done.3.tri_ref = bf16[128,16,256]{2,1,0:T(8,128)(2,1)} async-done(((bf16[128,16,256]{2,1,0:T(8,128)(2,1)}), bf16[128,16,256]{2,1,0:T(8,128)(2,1)}, u32[]{:S(2)}, u32[]{:S(2)}) %all-to-all-start.3) | async-done | bytes 1048608 | tf_op jit(solution)/shard_map/all_to_all | solution.py:321
  233.4 5.8 %last.1 = bf16[16,256,128]{2,1,0:T(8,128)(2,1)} custom-call(bf16[128,16,256]{2,1,0:T(8,128)(2,1)} %all-to-all-done.3.tri_ref, bf16[16,128,256]{2,1,0:T(8,128)(2,1)S(1)} %get-tuple-element.12.z_ref, f32[16,128,256]{2,1,0:T(8,128)S(1)} %gate_turned.1.gate_ref, bf16[128,128]{1,0:T(8,128)(2,1)S(1)} %get-tuple-element.15.w_out_ref), custom_call_target="tpu_custom_call" | custom-call | tf_op jit(solution)/shard_map/last/pallas_call | solution.py:306
  (15 shorter events, 0.9 us)
Async XLA Ops:
  1.0 1.2 copy-start.1
  9.2 1.3 copy-start
  10.5 64.6 %all-to-all-start = ((bf16[128,32,256]{2,1,0:T(8,128)(2,1)}), bf16[128,32,256]{2,1,0:T(8,128)(2,1)S(1)}, u32[]{:S(2)}, u32[]{:S(2)}) async-start(bf16[128,32,256]{2,1,0:T(8,128)(2,1)} %copy-done), calls=%async_computation | async-start | bytes 4194304 | tf_op jit(solution)/shard_map/all_to_all | solution.py:321
  75.8 6.4 %collective-permute-start = (bf16[64,2,16,256]{3,2,1,0:T(8,128)(2,1)S(1)}, bf16[64,2,16,256]{3,2,1,0:T(8,128)(2,1)S(1)}, u32[]{:S(2)}, u32[]{:S(2)}) collective-permute-start(bf16[64,2,16,256]{3,2,1,0:T(8,128)(2,1)S(1)} %outgoing.2), channel_id=1, source_target_pairs={{0,1},{1,0},{2,3},{3,2},{4,5},{5,4},{6,7},{7,6},{8,9},{9,8},{10,11... | collective-permute-start | bytes 3145736 | tf_op jit(solution)/shard_map/ppermute | solution.py:182
  84.0 8.2 %copy-start.6 = (bf16[2,128,128]{2,1,0:T(8,128)(2,1)S(1)}, bf16[2,128,128]{2,1,0:T(8,128)(2,1)}, u32[]{:S(2)}) copy-start(bf16[2,128,128]{2,1,0:T(8,128)(2,1)} %param.6) | copy-start | bytes 196612
  84.0 8.2 %copy-start.2 = (bf16[16,256,128]{2,1,0:T(8,128)(2,1)S(1)}, bf16[16,256,128]{2,1,0:T(8,128)(2,1)}, u32[]{:S(2)}) copy-start(bf16[16,256,128]{2,1,0:T(8,128)(2,1)} %pair_ref.3) | copy-start | bytes 3145732
  84.0 13.4 %copy-start.7 = (bf16[2,128,128]{2,1,0:T(8,128)(2,1)S(1)}, bf16[2,128,128]{2,1,0:T(8,128)(2,1)}, u32[]{:S(2)}) copy-start(bf16[2,128,128]{2,1,0:T(8,128)(2,1)} %param.7) | copy-start | bytes 196612
  84.0 35.8 %all-to-all-start.1 = ((bf16[128,16,256]{2,1,0:T(8,128)(2,1)}), bf16[128,16,256]{2,1,0:T(8,128)(2,1)S(1)}, u32[]{:S(2)}, u32[]{:S(2)}) async-start(bf16[128,16,256]{2,1,0:T(8,128)(2,1)} %bitcast.4), calls=%async_computation.1 | async-start | bytes 2097152 | tf_op jit(solution)/shard_map/all_to_all | solution.py:321
  95.1 1.3 copy-start.3
  96.4 1.0 copy-start.4
  119.8 1.2 copy-start.5
  187.9 7.4 %collective-permute-start.1 = (bf16[64,2,16,256]{3,2,1,0:T(8,128)(2,1)S(1)}, bf16[64,2,16,256]{3,2,1,0:T(8,128)(2,1)S(1)}, u32[]{:S(2)}, u32[]{:S(2)}) collective-permute-start(bf16[64,2,16,256]{3,2,1,0:T(8,128)(2,1)S(1)} %slice.28), channel_id=1, source_target_pairs={{0,1},{1,0},{2,3},{3,2},{4,5},{5,4},{6,7},{7,6},{8,9},{9,8},{10,11... | collective-permute-start | bytes 3145736 | tf_op jit(solution)/shard_map/ppermute | solution.py:207
  197.5 35.9 %all-to-all-start.3 = ((bf16[128,16,256]{2,1,0:T(8,128)(2,1)}), bf16[128,16,256]{2,1,0:T(8,128)(2,1)}, u32[]{:S(2)}, u32[]{:S(2)}) async-start(bf16[128,16,256]{2,1,0:T(8,128)(2,1)} %bitcast.9), calls=%async_computation.3 | async-start | bytes 2097152 | tf_op jit(solution)/shard_map/all_to_all | solution.py:321

commit v2 on v1

--- a/solution.py
+++ b/solution.py
@@ -15,7 +15,7 @@
 
 
 def params():
-    return pltpu.CompilerParams(vmem_limit_bytes=48 * 1024 * 1024)
+    return pltpu.CompilerParams(vmem_limit_bytes=24 * 1024 * 1024)
 
 
 def sigmoid(v):
@@ -37,41 +37,40 @@
     return jnp.dot(a, b, preferred_element_type=F32)
 
 
-def project(x, w_t, r, rows, wide, hidden):
+def project(x, w_t, r, sides, hidden):
     proj = dot(w_t, x)
-    left = sigmoid(proj[hidden : 2 * hidden]) * proj[:hidden]
-    right = sigmoid(proj[3 * hidden :]) * proj[2 * hidden : 3 * hidden]
-    for half in range(wide.shape[0]):
-        cols = slice(half * 128, half * 128 + 128)
-        wide[half, pl.ds(r, hidden, stride=2 * rows), :] = left[:, cols]
-        wide[half, pl.ds(rows + r, hidden, stride=2 * rows), :] = right[:, cols]
-
-
-def pack(wide, out_ref):
-    hidden, depth, _ = out_ref.shape
-
-    def step(c, _):
-        for half in range(wide.shape[0]):
-            rows = wide[half, pl.ds(pl.multiple_of(c * 8 * depth, 8 * depth), 8 * depth), :]
-            out_ref[pl.ds(c * 8, 8), :, half * 128 : half * 128 + 128] = rows.reshape(
-                8, depth, 128
-            ).astype(BF16)
-        return 0
-
-    lax.fori_loop(0, hidden // 8, step, 0)
-
-
-def first_kernel(pair_ref, w_in_ref, out_ref, wide, w_t):
+    for side in range(2):
+        at = 2 * side * hidden
+        gates = sigmoid(proj[at + hidden : at + 2 * hidden])
+        sides[side, r] = (gates * proj[at : at + hidden]).astype(BF16)
+
+
+def by_channel(sides, out_ref):
+    _, rows, hidden, cols = sides.shape
+    for side in range(2):
+        for lane in range(0, cols, 128):
+            for c in range(0, hidden, 32):
+                block = sides[side, :, c : c + 32, lane : lane + 128]
+                out_ref[c : c + 32, side * rows : side * rows + rows, lane : lane + 128] = (
+                    jnp.swapaxes(block, 0, 1)
+                )
+
+
+def by_row(tri_ref, tri):
+    hidden, _, cols = tri_ref.shape
+    for lane in range(0, cols, 128):
+        for c in range(0, hidden, 32):
+            block = tri_ref[c : c + 32, :, lane : lane + 128]
+            tri[:, c : c + 32, lane : lane + 128] = jnp.swapaxes(block, 0, 1)
+
+
+def first_kernel(pair_ref, w_in_ref, out_ref, sides, w_t):
     rows, _, hidden = pair_ref.shape
-    w_t[...] = turned(w_in_ref[...])
-
-    def step(r, _):
+    w_t[...] = turned(w_in_ref[0])
+    for r in range(rows):
         x = norm(pair_ref[r].astype(F32).T).astype(BF16)
-        project(x, w_t[...], r, rows, wide, hidden)
-        return 0
-
-    lax.fori_loop(0, rows, step, 0, unroll=2)
-    pack(wide, out_ref)
+        project(x, w_t[...], r, sides, hidden)
+    by_channel(sides, out_ref)
 
 
 def first(pair, w_in):
@@ -82,8 +81,8 @@
         in_specs=[VMEM, VMEM],
         out_specs=VMEM,
         scratch_shapes=[
-            pltpu.VMEM((cols // 128, hidden * 2 * rows, 128), F32),
-            pltpu.VMEM((w_in.shape[1], hidden), BF16),
+            pltpu.VMEM((2, rows, hidden, cols), BF16),
+            pltpu.VMEM((w_in.shape[2], hidden), BF16),
         ],
         compiler_params=params(),
         name="first",
@@ -91,17 +90,11 @@
 
 
 def gate_kernel(pair_ref, w_gate_ref, z_ref, gate_ref, w_t):
-    rows = pair_ref.shape[0]
-    w_t[...] = turned(w_gate_ref[...])
-
-    def step(r, _):
+    w_t[...] = turned(w_gate_ref[0])
+    for r in range(pair_ref.shape[0]):
         z = pair_ref[r].astype(F32).T
-        x = norm(z).astype(BF16)
         z_ref[r] = z.astype(BF16)
-        gate_ref[r] = sigmoid(dot(w_t[...], x))
-        return 0
-
-    lax.fori_loop(0, rows, step, 0, unroll=2)
+        gate_ref[r] = sigmoid(dot(w_t[...], norm(z).astype(BF16)))
 
 
 def gate(pair, w_gate):
@@ -121,14 +114,9 @@
 
 
 def gate_turned_kernel(z_ref, w_gate_ref, gate_ref, w_t):
-    w_t[...] = turned(w_gate_ref[...])
-
-    def step(r, _):
-        x = norm(z_ref[r].astype(F32)).astype(BF16)
-        gate_ref[r] = sigmoid(dot(w_t[...], x))
-        return 0
-
-    lax.fori_loop(0, z_ref.shape[0], step, 0, unroll=2)
+    w_t[...] = turned(w_gate_ref[1])
+    for r in range(z_ref.shape[0]):
+        gate_ref[r] = sigmoid(dot(w_t[...], norm(z_ref[r].astype(F32)).astype(BF16)))
 
 
 def gate_turned(z, w_gate):
@@ -216,55 +204,23 @@
     return out.reshape(src, depth // 2, cols)
 
 
-def normed_rows(tri_ref, flat):
-    hidden, rows, cols = tri_ref.shape
-    for half in range(cols // 128):
-        lanes = slice(half * 128, half * 128 + 128)
-        zero = jnp.zeros((rows, 128), F32)
-
-        def add(c, total):
-            return total + tri_ref[c, :, lanes].astype(F32)
-
-        mean = lax.fori_loop(0, hidden, add, zero, unroll=8) * (1.0 / hidden)
-
-        def square(c, total):
-            centred = tri_ref[c, :, lanes].astype(F32) - mean
-            return total + centred * centred
-
-        var = lax.fori_loop(0, hidden, square, zero, unroll=8) * (1.0 / hidden)
-        scale = lax.rsqrt(var + 1e-05)
-
-        def write(c, _):
-            flat[half, pl.ds(pl.multiple_of(c * rows, rows), rows), :] = (
-                tri_ref[c, :, lanes].astype(F32) - mean
-            ) * scale
-            return 0
-
-        lax.fori_loop(0, hidden, write, 0, unroll=8)
-
-
-def row_of(flat, r, hidden, rows):
-    return jnp.concatenate(
-        [flat[half, pl.ds(r, hidden, stride=rows), :] for half in range(flat.shape[0])], axis=1
-    ).astype(BF16)
-
-
-def middle_kernel(tri_ref, z_ref, gate_ref, w_out_ref, w_in_ref, out_ref, z_new_ref, flat, wide, w_out_t, w_in_t):
+def updated(tri, z_ref, gate_ref, w_out_t, r):
+    y = norm(tri[r].astype(F32)).astype(BF16)
+    return z_ref[r].astype(F32) + gate_ref[r] * dot(w_out_t[...], y)
+
+
+def middle_kernel(
+    tri_ref, z_ref, gate_ref, w_out_ref, w_in_ref, out_ref, z_new_ref, tri, sides, w_out_t, w_in_t
+):
     hidden, rows, _ = tri_ref.shape
-    w_out_t[...] = turned(w_out_ref[...])
-    w_in_t[...] = turned(w_in_ref[...])
-    normed_rows(tri_ref, flat)
-
-    def step(r, _):
-        update = gate_ref[r] * dot(w_out_t[...], row_of(flat, r, hidden, rows))
-        z = (z_ref[r].astype(F32) + update).astype(BF16)
+    w_out_t[...] = turned(w_out_ref[0])
+    w_in_t[...] = turned(w_in_ref[1])
+    by_row(tri_ref, tri)
+    for r in range(rows):
+        z = updated(tri, z_ref, gate_ref, w_out_t, r).astype(BF16)
         z_new_ref[r] = z
-        x = norm(z.astype(F32)).astype(BF16)
-        project(x, w_in_t[...], r, rows, wide, hidden)
-        return 0
-
-    lax.fori_loop(0, rows, step, 0, unroll=2)
-    pack(wide, out_ref)
+        project(norm(z.astype(F32)).astype(BF16), w_in_t[...], r, sides, hidden)
+    by_channel(sides, out_ref)
 
 
 def middle(tri, z, gates, w_out, w_in):
@@ -278,27 +234,21 @@
         in_specs=[VMEM] * 5,
         out_specs=(VMEM, VMEM),
         scratch_shapes=[
-            pltpu.VMEM((cols // 128, hidden * rows, 128), F32),
-            pltpu.VMEM((cols // 128, hidden * 2 * rows, 128), F32),
+            pltpu.VMEM((rows, hidden, cols), BF16),
+            pltpu.VMEM((2, rows, hidden, cols), BF16),
             pltpu.VMEM((hidden, hidden), BF16),
-            pltpu.VMEM((w_in.shape[1], hidden), BF16),
+            pltpu.VMEM((w_in.shape[2], hidden), BF16),
         ],
         compiler_params=params(),
         name="middle",
     )(tri, z, gates, w_out, w_in)
 
 
-def last_kernel(tri_ref, z_ref, gate_ref, w_out_ref, out_ref, flat, w_out_t):
-    hidden, rows, _ = tri_ref.shape
-    w_out_t[...] = turned(w_out_ref[...])
-    normed_rows(tri_ref, flat)
-
-    def step(r, _):
-        update = gate_ref[r] * dot(w_out_t[...], row_of(flat, r, hidden, rows))
-        out_ref[r] = (z_ref[r].astype(F32) + update).T.astype(BF16)
-        return 0
-
-    lax.fori_loop(0, rows, step, 0, unroll=2)
+def last_kernel(tri_ref, z_ref, gate_ref, w_out_ref, out_ref, tri, w_out_t):
+    w_out_t[...] = turned(w_out_ref[1])
+    by_row(tri_ref, tri)
+    for r in range(tri_ref.shape[1]):
+        out_ref[r] = updated(tri, z_ref, gate_ref, w_out_t, r).T.astype(BF16)
 
 
 def last(tri, z, gates, w_out):
@@ -309,7 +259,7 @@
         in_specs=[VMEM] * 4,
         out_specs=VMEM,
         scratch_shapes=[
-            pltpu.VMEM((cols // 128, hidden * rows, 128), F32),
+            pltpu.VMEM((rows, hidden, cols), BF16),
             pltpu.VMEM((hidden, hidden), BF16),
         ],
         compiler_params=params(),
@@ -323,14 +273,14 @@
 
 def on_device(pair, w_in, w_gate, w_out):
     core = lax.axis_index("core")
-    z, gates = gate(pair, w_gate[0])
-    got = exchange(first(pair, w_in[0]))
+    z, gates = gate(pair, w_gate)
+    got = exchange(first(pair, w_in))
     tri = exchange(outgoing(got, core))
-    sent, z = middle(tri, z, gates, w_out[0], w_in[1])
-    gates = gate_turned(z, w_gate[1])
+    sent, z = middle(tri, z, gates, w_out, w_in)
+    gates = gate_turned(z, w_gate)
     got = exchange(sent)
     tri = exchange(incoming(got, core))
-    return last(tri, z, gates, w_out[1])
+    return last(tri, z, gates, w_out)
 
 
 def solution(mesh):

time: 241 us -> 230 us (0.954)
  Pallas kernels: 33.5 us -> 17.6 us
  waiting for transfers between devices: 100 us -> 103 us
    pallas_call x1, Pallas kernels: 10.9 us -> 4.41 us  [middle(): pl.pallas_call(middle_kernel, out_shape=(jax.ShapeDtypeStruct((hidden, 2...]
    pallas_call x1, Pallas kernels: 6.97 us -> 2.57 us  [first(): pl.pallas_call(first_kernel, out_shape=jax.ShapeDtypeStruct((hidden, 2 *...]
    unnamed x16 -> x22, local copies, waits for them, and re-layouts: 6.1 us -> 8.65 us
    all_to_all x3, waiting for transfers between devices: 95.5 us -> 98 us  [exchange(): lax.all_to_all(blocks, CHIPS, split_axis=0, concat_axis=0, tiled=True)]
  transfers between devices with their start and end apart: 5 -> 5, of which waited for: 5 -> 5; matrix products, arithmetic and copies ran while one was open for 0% -> 0% of each run, Pallas kernels for 2% -> 1%
where the time goes in v2:
time: 230 us; the launch traced here: 228 us
  waiting for transfers between devices  103 us (45%)
  blocking collectives  55.9 us (24%)
  starting transfers between devices  42.9 us (19%)
  Pallas kernels  17.6 us (8%)
  local copies, waits for them, and re-layouts  8.77 us (4%)
    all_to_all x3, waiting for transfers between devices, exchange(): lax.all_to_all(blocks, CHIPS, split_axis=0, concat_axis=0, tiled=True)  98 us
    all_to_all x1, blocking collectives, exchange(): lax.all_to_all(blocks, CHIPS, split_axis=0, concat_axis=0, tiled=True)  55.9 us
    all_to_all x3, starting transfers between devices, exchange(): lax.all_to_all(blocks, CHIPS, split_axis=0, concat_axis=0, tiled=True)  33.7 us
    unnamed x22, local copies, waits for them, and re-layouts  8.65 us
    ppermute x1, starting transfers between devices, incoming(): left = lax.ppermute(got[:, :, :depth // 2], 'core', [(0, 1), (1, 0)])  5.12 us
  transfers between devices with their start and end apart: 5, of which 5 were waited for; matrix products, arithmetic and copies ran while one was open for 0% of the time, Pallas kernels for 1%

profile of v2, /device:TPU:1, one launch (start us, length us, event | category | flops | bytes accessed | tf_op | source)
XLA Modules:
  0.0 227.8 jit_solution(10914130942903886790)
XLA Ops:
  0.0 1.2 copy-done.1
  2.2 2.6 %first.1 = bf16[128,32,256]{2,1,0:T(8,128)(2,1)S(1)} custom-call(bf16[16,256,128]{2,1,0:T(8,128)(2,1)S(1)} %copy-done.1, bf16[2,128,512]{2,1,0:T(8,128)(2,1)S(1)} %copy-done.7), custom_call_target="tpu_custom_call" | custom-call | tf_op jit(solution)/shard_map/first/pallas_call | solution.py:78
  4.8 1.3 copy-done
  6.1 16.4 %all-to-all-start = ((bf16[128,32,256]{2,1,0:T(8,128)(2,1)}), bf16[128,32,256]{2,1,0:T(8,128)(2,1)S(1)}, u32[]{:S(2)}, u32[]{:S(2)}) async-start(bf16[128,32,256]{2,1,0:T(8,128)(2,1)} %copy-done), calls=%async_computation | async-start | bytes 4194304 | tf_op jit(solution)/shard_map/all_to_all | solution.py:271
  22.5 48.2 %all-to-all-done = bf16[128,32,256]{2,1,0:T(8,128)(2,1)S(1)} async-done(((bf16[128,32,256]{2,1,0:T(8,128)(2,1)}), bf16[128,32,256]{2,1,0:T(8,128)(2,1)S(1)}, u32[]{:S(2)}, u32[]{:S(2)}) %all-to-all-start) | async-done | bytes 2097184 | tf_op jit(solution)/shard_map/all_to_all | solution.py:271
  71.4 4.1 %collective-permute-start = (bf16[64,2,16,256]{3,2,1,0:T(8,128)(2,1)S(1)}, bf16[64,2,16,256]{3,2,1,0:T(8,128)(2,1)S(1)}, u32[]{:S(2)}, u32[]{:S(2)}) collective-permute-start(bf16[64,2,16,256]{3,2,1,0:T(8,128)(2,1)S(1)} %outgoing.2), channel_id=1, source_target_pairs={{0,1},{1,0},{2,3},{3,2},{4,5},{5,4},{6,7},{7,6},{8,9},{9,8},{10,11... | collective-permute-start | bytes 3145736 | tf_op jit(solution)/shard_map/ppermute | solution.py:170
  75.5 2.3 %collective-permute-done.refs_0_ = bf16[64,2,16,256]{3,2,1,0:T(8,128)(2,1)S(1)} collective-permute-done((bf16[64,2,16,256]{3,2,1,0:T(8,128)(2,1)S(1)}, bf16[64,2,16,256]{3,2,1,0:T(8,128)(2,1)S(1)}, u32[]{:S(2)}, u32[]{:S(2)}) %collective-permute-start) | collective-permute-done | bytes 1048608 | tf_op jit(solution)/shard_map/ppermute | solution.py:170
  77.8 1.7 outgoing.3
  79.5 8.4 %all-to-all-start.1 = ((bf16[128,16,256]{2,1,0:T(8,128)(2,1)}), bf16[128,16,256]{2,1,0:T(8,128)(2,1)S(1)}, u32[]{:S(2)}, u32[]{:S(2)}) async-start(bf16[128,16,256]{2,1,0:T(8,128)(2,1)} %bitcast.3), calls=%async_computation.1 | async-start | bytes 2097152 | tf_op jit(solution)/shard_map/all_to_all | solution.py:271
  88.0 1.2 gate.1
  89.2 1.3 copy-done.3
  90.5 1.0 copy-done.5
  91.5 23.9 %all-to-all-done.1.tri_ref = bf16[128,16,256]{2,1,0:T(8,128)(2,1)S(1)} async-done(((bf16[128,16,256]{2,1,0:T(8,128)(2,1)}), bf16[128,16,256]{2,1,0:T(8,128)(2,1)S(1)}, u32[]{:S(2)}, u32[]{:S(2)}) %all-to-all-start.1) | async-done | bytes 1048608 | tf_op jit(solution)/shard_map/all_to_all | solution.py:271
  115.4 1.6 copy-done.4
  117.0 1.2 copy-done.6
  118.2 4.4 %middle.1 = (bf16[128,32,256]{2,1,0:T(8,128)(2,1)S(1)}, bf16[16,128,256]{2,1,0:T(8,128)(2,1)S(1)}) custom-call(bf16[128,16,256]{2,1,0:T(8,128)(2,1)S(1)} %all-to-all-done.1.tri_ref, bf16[16,128,256]{2,1,0:T(8,128)(2,1)S(1)} %copy-done.6, f32[16,128,256]{2,1,0:T(8,128)S(1)} %copy-done.4, bf16[2,128,128]{2,1,0:T(8,128)(2,1)S(1)} %copy-done.10, ...), custom_call_target="tpu_custom_call" | custom-call | tf_op jit(solution)/shard_map/middle/pallas_call | solution.py:228
  122.6 55.9 %all_to_all.20 = bf16[128,32,256]{2,1,0:T(8,128)(2,1)S(1)} all-to-all(bf16[128,32,256]{2,1,0:T(8,128)(2,1)S(1)} %get-tuple-element.11), channel_id=1, replica_groups=mesh['z'=8,'x'=4,'yl'=2,'yh'=2,'core'=2] {'z','x','yl','yh'}, dimensions={0} | all-to-all | bytes 4194304 | tf_op jit(solution)/shard_map/all_to_all | solution.py:271
  178.6 5.1 %collective-permute-start.1 = (bf16[64,2,16,256]{3,2,1,0:T(8,128)(2,1)S(1)}, bf16[64,2,16,256]{3,2,1,0:T(8,128)(2,1)S(1)}, u32[]{:S(2)}, u32[]{:S(2)}) collective-permute-start(bf16[64,2,16,256]{3,2,1,0:T(8,128)(2,1)S(1)} %slice.4), channel_id=1, source_target_pairs={{0,1},{1,0},{2,3},{3,2},{4,5},{5,4},{6,7},{7,6},{8,9},{9,8},{10,11... | collective-permute-start | bytes 3145736 | tf_op jit(solution)/shard_map/ppermute | solution.py:195
  183.7 2.3 %collective-permute-done.1.left_ref = bf16[64,2,16,256]{3,2,1,0:T(8,128)(2,1)S(1)} collective-permute-done((bf16[64,2,16,256]{3,2,1,0:T(8,128)(2,1)S(1)}, bf16[64,2,16,256]{3,2,1,0:T(8,128)(2,1)S(1)}, u32[]{:S(2)}, u32[]{:S(2)}) %collective-permute-start.1) | collective-permute-done | bytes 1048608 | tf_op jit(solution)/shard_map/ppermute | solution.py:195
  186.0 2.2 incoming.1
  188.3 8.9 %all-to-all-start.3 = ((bf16[128,16,256]{2,1,0:T(8,128)(2,1)}), bf16[128,16,256]{2,1,0:T(8,128)(2,1)}, u32[]{:S(2)}, u32[]{:S(2)}) async-start(bf16[128,16,256]{2,1,0:T(8,128)(2,1)} %bitcast.5), calls=%async_computation.3 | async-start | bytes 2097152 | tf_op jit(solution)/shard_map/all_to_all | solution.py:271
  197.2 1.0 gate_turned.1.gate_ref
  198.2 25.9 %all-to-all-done.3.tri_ref = bf16[128,16,256]{2,1,0:T(8,128)(2,1)} async-done(((bf16[128,16,256]{2,1,0:T(8,128)(2,1)}), bf16[128,16,256]{2,1,0:T(8,128)(2,1)}, u32[]{:S(2)}, u32[]{:S(2)}) %all-to-all-start.3) | async-done | bytes 1048608 | tf_op jit(solution)/shard_map/all_to_all | solution.py:271
  224.1 3.7 %last.1 = bf16[16,256,128]{2,1,0:T(8,128)(2,1)} custom-call(bf16[128,16,256]{2,1,0:T(8,128)(2,1)} %all-to-all-done.3.tri_ref, bf16[16,128,256]{2,1,0:T(8,128)(2,1)S(1)} %get-tuple-element.12.z_ref, f32[16,128,256]{2,1,0:T(8,128)S(1)} %gate_turned.1.gate_ref, bf16[2,128,128]{2,1,0:T(8,128)(2,1)S(1)} %copy-done.10), custom_call_target="tpu_custom_call" | custom-call | tf_op jit(solution)/shard_map/last/pallas_call | solution.py:256
  (18 shorter events, 1.8 us)
Async XLA Ops:
  0.0 1.2 copy-start.1
  1.2 0.9 copy-start.7
  4.8 1.3 copy-start
  6.1 64.6 %all-to-all-start = ((bf16[128,32,256]{2,1,0:T(8,128)(2,1)}), bf16[128,32,256]{2,1,0:T(8,128)(2,1)S(1)}, u32[]{:S(2)}, u32[]{:S(2)}) async-start(bf16[128,32,256]{2,1,0:T(8,128)(2,1)} %copy-done), calls=%async_computation | async-start | bytes 4194304 | tf_op jit(solution)/shard_map/all_to_all | solution.py:271
  71.4 6.4 %collective-permute-start = (bf16[64,2,16,256]{3,2,1,0:T(8,128)(2,1)S(1)}, bf16[64,2,16,256]{3,2,1,0:T(8,128)(2,1)S(1)}, u32[]{:S(2)}, u32[]{:S(2)}) collective-permute-start(bf16[64,2,16,256]{3,2,1,0:T(8,128)(2,1)S(1)} %outgoing.2), channel_id=1, source_target_pairs={{0,1},{1,0},{2,3},{3,2},{4,5},{5,4},{6,7},{7,6},{8,9},{9,8},{10,11... | collective-permute-start | bytes 3145736 | tf_op jit(solution)/shard_map/ppermute | solution.py:170
  79.5 8.4 %copy-start.2 = (bf16[16,256,128]{2,1,0:T(8,128)(2,1)S(1)}, bf16[16,256,128]{2,1,0:T(8,128)(2,1)}, u32[]{:S(2)}) copy-start(bf16[16,256,128]{2,1,0:T(8,128)(2,1)} %pair_ref.3) | copy-start | bytes 3145732
  79.5 8.4 %copy-start.9 = (bf16[2,128,128]{2,1,0:T(8,128)(2,1)S(1)}, bf16[2,128,128]{2,1,0:T(8,128)(2,1)}, u32[]{:S(2)}) copy-start(bf16[2,128,128]{2,1,0:T(8,128)(2,1)} %w_gate_ref.3) | copy-start | bytes 196612
  79.5 35.8 %copy-start.8 = (bf16[2,128,512]{2,1,0:T(8,128)(2,1)S(1)}, bf16[2,128,512]{2,1,0:T(8,128)(2,1)}, u32[]{:S(2)}) copy-start(bf16[2,128,512]{2,1,0:T(8,128)(2,1)} %w_in_ref.3) | copy-start | bytes 786436
  79.5 35.8 %copy-start.10 = (bf16[2,128,128]{2,1,0:T(8,128)(2,1)S(1)}, bf16[2,128,128]{2,1,0:T(8,128)(2,1)}, u32[]{:S(2)}) copy-start(bf16[2,128,128]{2,1,0:T(8,128)(2,1)} %w_out_ref.3) | copy-start | bytes 196612
  79.5 35.8 %all-to-all-start.1 = ((bf16[128,16,256]{2,1,0:T(8,128)(2,1)}), bf16[128,16,256]{2,1,0:T(8,128)(2,1)S(1)}, u32[]{:S(2)}, u32[]{:S(2)}) async-start(bf16[128,16,256]{2,1,0:T(8,128)(2,1)} %bitcast.3), calls=%async_computation.1 | async-start | bytes 2097152 | tf_op jit(solution)/shard_map/all_to_all | solution.py:271
  89.2 1.3 copy-start.3
  90.5 1.0 copy-start.5
  115.4 1.6 copy-start.4
  117.0 1.2 copy-start.6
  178.6 7.4 %collective-permute-start.1 = (bf16[64,2,16,256]{3,2,1,0:T(8,128)(2,1)S(1)}, bf16[64,2,16,256]{3,2,1,0:T(8,128)(2,1)S(1)}, u32[]{:S(2)}, u32[]{:S(2)}) collective-permute-start(bf16[64,2,16,256]{3,2,1,0:T(8,128)(2,1)S(1)} %slice.4), channel_id=1, source_target_pairs={{0,1},{1,0},{2,3},{3,2},{4,5},{5,4},{6,7},{7,6},{8,9},{9,8},{10,11... | collective-permute-start | bytes 3145736 | tf_op jit(solution)/shard_map/ppermute | solution.py:195
  188.3 35.9 %all-to-all-start.3 = ((bf16[128,16,256]{2,1,0:T(8,128)(2,1)}), bf16[128,16,256]{2,1,0:T(8,128)(2,1)}, u32[]{:S(2)}, u32[]{:S(2)}) async-start(bf16[128,16,256]{2,1,0:T(8,128)(2,1)} %bitcast.5), calls=%async_computation.3 | async-start | bytes 2097152 | tf_op jit(solution)/shard_map/all_to_all | solution.py:271

commit v3 on v2

v3 whole, which is shorter than its diff:
```python
import jax
import jax.numpy as jnp
from jax import lax
from jax.experimental import pallas as pl
from jax.experimental.pallas import tpu as pltpu
from jax.sharding import Mesh, PartitionSpec as P

AXES = ("z", "x", "yl", "yh", "core")
CHIPS = ("z", "x", "yl", "yh")
F32, BF16 = jnp.float32, jnp.bfloat16
VMEM = pl.BlockSpec(memory_space=pltpu.VMEM)
SMEM = pl.BlockSpec(memory_space=pltpu.SMEM)
HBM = pl.BlockSpec(memory_space=pltpu.HBM)


def params():
    return pltpu.CompilerParams(vmem_limit_bytes=24 * 1024 * 1024)


def sigmoid(v):
    return 0.5 * jnp.tanh(0.5 * v) + 0.5


def norm(v):
    mean = jnp.mean(v, axis=0, keepdims=True)
    centred = v - mean
    var = jnp.mean(centred * centred, axis=0, keepdims=True)
    return centred * lax.rsqrt(var + 1e-05)


def turned(w):
    return w.astype(F32).T.astype(BF16)


def dot(a, b):
    return jnp.dot(a, b, preferred_element_type=F32)


def project(x, w_t, r, sides, hidden):
    proj = dot(w_t, x)
    for side in range(2):
        at = 2 * side * hidden
        gates = sigmoid(proj[at + hidden : at + 2 * hidden])
        sides[side, r] = (gates * proj[at : at + hidden]).astype(BF16)


def by_channel(sides, out_ref):
    _, rows, hidden, cols = sides.shape
    for side in range(2):
        for lane in range(0, cols, 128):
            for c in range(0, hidden, 32):
                block = sides[side, :, c : c + 32, lane : lane + 128]
                out_ref[c : c + 32, side * rows : side * rows + rows, lane : lane + 128] = (
                    jnp.swapaxes(block, 0, 1)
                )


def by_row(tri_ref, tri):
    hidden, _, cols = tri_ref.shape
    for lane in range(0, cols, 128):
        for c in range(0, hidden, 32):
            block = tri_ref[c : c + 32, :, lane : lane + 128]
            tri[:, c : c + 32, lane : lane + 128] = jnp.swapaxes(block, 0, 1)


def first_kernel(pair_ref, w_in_ref, out_ref, sides, w_t):
    rows, _, hidden = pair_ref.shape
    w_t[...] = turned(w_in_ref[0])
    for r in range(rows):
        x = norm(pair_ref[r].astype(F32).T).astype(BF16)
        project(x, w_t[...], r, sides, hidden)
    by_channel(sides, out_ref)


def first(pair, w_in):
    rows, cols, hidden = pair.shape
    return pl.pallas_call(
        first_kernel,
        out_shape=jax.ShapeDtypeStruct((hidden, 2 * rows, cols), BF16),
        in_specs=[VMEM, VMEM],
        out_specs=VMEM,
        scratch_shapes=[
            pltpu.VMEM((2, rows, hidden, cols), BF16),
            pltpu.VMEM((w_in.shape[2], hidden), BF16),
        ],
        compiler_params=params(),
        name="first",
    )(pair, w_in)


def products(got_ref, yo, core):
    blocks, _, depth, cols = got_ref.shape
    rows = depth // 2
    per = cols // rows
    total = None
    for yk in range(2):
        a = got_ref[:, yk, :rows, :].reshape(blocks * rows, cols)
        b = got_ref[pl.ds((yo * 2 + core) * per, per), yk, rows:, :].reshape(cols, cols)
        part = lax.dot_general(a, b, (((1,), (1,)), ((), ())), preferred_element_type=F32)
        total = part if total is None else total + part
    return total.reshape(blocks, rows, cols)


def other_kernel(core_ref, got_ref, out_ref):
    for yo in range(2):
        out_ref[:, yo] = products(got_ref, yo, 1 - core_ref[0]).astype(BF16)


def own_kernel(core_ref, got_ref, pair_ref, w_gate_ref, own_ref, z_ref, gate_ref, w_t):
    for yo in range(2):
        own_ref[:, yo] = products(got_ref, yo, core_ref[0])
    w_t[...] = turned(w_gate_ref[0])
    for r in range(pair_ref.shape[0]):
        z = pair_ref[r].astype(F32).T
        z_ref[r] = z.astype(BF16)
        gate_ref[r] = sigmoid(dot(w_t[...], norm(z).astype(BF16)))


def sum_kernel(own_ref, other_ref, out_ref):
    out_ref[...] = (own_ref[...] + other_ref[...].astype(F32)).astype(BF16)


def outgoing(got, core, pair, w_gate):
    src, depth, cols = got.shape
    rows, _, hidden = pair.shape
    got = got.reshape(src // 2, 2, depth, cols)
    tri = (src // 2, 2, depth // 2, cols)
    other = pl.pallas_call(
        other_kernel,
        out_shape=jax.ShapeDtypeStruct(tri, BF16),
        in_specs=[SMEM, VMEM],
        out_specs=VMEM,
        compiler_params=params(),
        name="other",
    )(core, got)
    other = lax.ppermute(other, "core", [(0, 1), (1, 0)])
    own, z, gates = pl.pallas_call(
        own_kernel,
        out_shape=(
            jax.ShapeDtypeStruct(tri, F32),
            jax.ShapeDtypeStruct((rows, hidden, cols), BF16),
            jax.ShapeDtypeStruct((rows, hidden, cols), F32),
        ),
        in_specs=[SMEM, VMEM, VMEM, VMEM],
        out_specs=(VMEM,) * 3,
        scratch_shapes=[pltpu.VMEM((hidden, hidden), BF16)],
        compiler_params=params(),
        name="own",
    )(core, got, pair, w_gate)
    summed = pl.pallas_call(
        sum_kernel,
        out_shape=jax.ShapeDtypeStruct(tri, BF16),
        in_specs=[VMEM, VMEM],
        out_specs=VMEM,
        compiler_params=params(),
        name="sum",
    )(own, other)
    return summed.reshape(src, depth // 2, cols), z, gates


def columns(left, got_ref, yo):
    blocks, _, depth, cols = got_ref.shape
    rows = depth // 2
    right = got_ref[:, yo, rows:, :].reshape(blocks * rows, cols)
    part = lax.dot_general(
        left.reshape(blocks * rows, cols),
        right,
        (((0,), (0,)), ((), ())),
        preferred_element_type=F32,
    )
    return part.reshape(cols // rows, rows, cols).astype(BF16)


def near_kernel(got_ref, z_ref, w_gate_ref, near_ref, gate_ref, w_t):
    rows = z_ref.shape[0]
    per = near_ref.shape[0] // 2
    for yi in range(2):
        for yo in range(2):
            near_ref[yi * per : yi * per + per, yo] = columns(got_ref[:, yi, :rows, :], got_ref, yo)
    w_t[...] = turned(w_gate_ref[1])
    for r in range(rows):
        gate_ref[r] = sigmoid(dot(w_t[...], norm(z_ref[r].astype(F32)).astype(BF16)))


def far_kernel(core_ref, got_ref, left_ref, near_ref, out_ref):
    per = near_ref.shape[0] // 2
    core = core_ref[0]
    for yi in range(2):
        out_ref[pl.ds((yi * 2 + core) * per, per)] = near_ref[yi * per : yi * per + per]
        for yo in range(2):
            out_ref[pl.ds((yi * 2 + 1 - core) * per, per), yo] = columns(left_ref[:, yi], got_ref, yo)


def incoming(got, core, z, w_gate):
    src, depth, cols = got.shape
    rows, hidden, _ = z.shape
    got = got.reshape(src // 2, 2, depth, cols)
    left = lax.ppermute(got[:, :, : depth // 2], "core", [(0, 1), (1, 0)])
    near, gates = pl.pallas_call(
        near_kernel,
        out_shape=(
            jax.ShapeDtypeStruct((2 * cols // rows, 2, rows, cols), BF16),
            jax.ShapeDtypeStruct((rows, hidden, cols), F32),
        ),
        in_specs=[VMEM, VMEM, VMEM],
        out_specs=(VMEM, VMEM),
        scratch_shapes=[pltpu.VMEM((hidden, hidden), BF16)],
        compiler_params=params(),
        name="near",
    )(got, z, w_gate)
    out = pl.pallas_call(
        far_kernel,
        out_shape=jax.ShapeDtypeStruct((src // 2, 2, depth // 2, cols), BF16),
        in_specs=[SMEM, VMEM, VMEM, VMEM],
        out_specs=VMEM,
        compiler_params=params(),
        name="far",
    )(core, got, left, near)
    return out.reshape(src, depth // 2, cols), gates


def updated(tri, z_ref, gate_ref, w_out_t, r):
    y = norm(tri[r].astype(F32)).astype(BF16)
    return z_ref[r].astype(F32) + gate_ref[r] * dot(w_out_t[...], y)


def middle_kernel(
    tri_ref, z_ref, gate_ref, w_out_ref, w_in_ref, out_ref, z_new_ref, tri, sides, w_out_t, w_in_t
):
    hidden, rows, _ = tri_ref.shape
    w_out_t[...] = turned(w_out_ref[0])
    w_in_t[...] = turned(w_in_ref[1])
    by_row(tri_ref, tri)
    for r in range(rows):
        z = updated(tri, z_ref, gate_ref, w_out_t, r).astype(BF16)
        z_new_ref[r] = z
        project(norm(z.astype(F32)).astype(BF16), w_in_t[...], r, sides, hidden)
    by_channel(sides, out_ref)


def middle(tri, z, gates, w_out, w_in):
    hidden, rows, cols = tri.shape
    return pl.pallas_call(
        middle_kernel,
        out_shape=(
            jax.ShapeDtypeStruct((hidden, 2 * rows, cols), BF16),
            jax.ShapeDtypeStruct((rows, hidden, cols), BF16),
        ),
        in_specs=[VMEM] * 5,
        out_specs=(VMEM, VMEM),
        scratch_shapes=[
            pltpu.VMEM((rows, hidden, cols), BF16),
            pltpu.VMEM((2, rows, hidden, cols), BF16),
            pltpu.VMEM((hidden, hidden), BF16),
            pltpu.VMEM((w_in.shape[2], hidden), BF16),
        ],
        compiler_params=params(),
        name="middle",
    )(tri, z, gates, w_out, w_in)


def last_kernel(tri_ref, z_ref, gate_ref, w_out_ref, out_ref, tri, rows_out, w_out_t, sems):
    w_out_t[...] = turned(w_out_ref[1])
    by_row(tri_ref, tri)
    copies = []
    for r in range(tri_ref.shape[1]):
        rows_out[r] = updated(tri, z_ref, gate_ref, w_out_t, r).T.astype(BF16)
        copies.append(pltpu.make_async_copy(rows_out.at[r], out_ref.at[r], sems.at[r]))
        copies[-1].start()
    for copy in copies:
        copy.wait()


def last(tri, z, gates, w_out):
    hidden, rows, cols = tri.shape
    return pl.pallas_call(
        last_kernel,
        out_shape=jax.ShapeDtypeStruct((rows, cols, hidden), BF16),
        in_specs=[VMEM] * 4,
        out_specs=HBM,
        scratch_shapes=[
            pltpu.VMEM((rows, hidden, cols), BF16),
            pltpu.VMEM((rows, cols, hidden), BF16),
            pltpu.VMEM((hidden, hidden), BF16),
            pltpu.SemaphoreType.DMA((rows,)),
        ],
        compiler_params=params(),
        name="last",
    )(tri, z, gates, w_out)


def exchange(blocks):
    return lax.all_to_all(blocks, CHIPS, split_axis=0, concat_axis=0, tiled=True)


def on_device(pair, w_in, w_gate, w_out):
    core = lax.axis_index("core").reshape(1)
    got = exchange(first(pair, w_in))
    tri, z, gates = outgoing(got, core, pair, w_gate)
    sent, z = middle(exchange(tri), z, gates, w_out, w_in)
    tri, gates = incoming(exchange(sent), core, z, w_gate)
    return last(exchange(tri), z, gates, w_out)


def solution(mesh):
    mesh = Mesh(mesh.devices.reshape(8, 4, 2, 2, 2), AXES)
    placed = P(("z", "x", "yl"), ("yh", "core"), None)
    return jax.shard_map(
        on_device, mesh=mesh, in_specs=(placed, P(), P(), P()), out_specs=placed, check_vma=False
    )
```

time: 230 us -> 222 us (0.965)
  blocking collectives: 55.9 us -> 127 us
  waiting for transfers between devices: 103 us -> 49.7 us
  starting transfers between devices: 42.9 us -> 25.6 us
  local copies, waits for them, and re-layouts: 8.77 us -> 3.65 us
  Pallas kernels: 17.6 us -> 14.1 us
    all_to_all x1 -> x3, blocking collectives: 55.9 us -> 127 us  [exchange(): lax.all_to_all(blocks, CHIPS, split_axis=0, concat_axis=0, tiled=True)]
    all_to_all x3 -> x1, waiting for transfers between devices: 98 us -> 48.2 us  [exchange(): lax.all_to_all(blocks, CHIPS, split_axis=0, concat_axis=0, tiled=True)]
    all_to_all x3 -> x1, starting transfers between devices: 33.7 us -> 16.4 us  [exchange(): lax.all_to_all(blocks, CHIPS, split_axis=0, concat_axis=0, tiled=True)]
    unnamed x22 -> x14, local copies, waits for them, and re-layouts: 8.65 us -> 3.52 us
  transfers between devices with their start and end apart: 5 -> 3, of which waited for: 5 -> 3; matrix products, arithmetic and copies ran while one was open for 0% -> 0% of each run, Pallas kernels for 1% -> 1%
where the time goes in v3:
time: 222 us; the launch traced here: 220 us
  blocking collectives  127 us (57%)
  waiting for transfers between devices  49.7 us (22%)
  starting transfers between devices  25.6 us (12%)
  Pallas kernels  14.1 us (6%)
  local copies, waits for them, and re-layouts  3.65 us (2%)
    all_to_all x3, blocking collectives, exchange(): lax.all_to_all(blocks, CHIPS, split_axis=0, concat_axis=0, tiled=True)  127 us
    all_to_all x1, waiting for transfers between devices, exchange(): lax.all_to_all(blocks, CHIPS, split_axis=0, concat_axis=0, tiled=True)  48.2 us
    all_to_all x1, starting transfers between devices, exchange(): lax.all_to_all(blocks, CHIPS, split_axis=0, concat_axis=0, tiled=True)  16.4 us
    ppermute x1, starting transfers between devices, incoming(): left = lax.ppermute(got[:, :, :depth // 2], 'core', [(0, 1), (1, 0)])  5.13 us
  transfers between devices with their start and end apart: 3, of which 3 were waited for; matrix products, arithmetic and copies ran while one was open for 0% of the time, Pallas kernels for 1%

profile of v3, /device:TPU:1, one launch (start us, length us, event | category | flops | bytes accessed | tf_op | source)
XLA Modules:
  0.0 220.3 jit_solution(8945011671627415102)
XLA Ops:
  0.0 1.2 copy-done.1
  1.2 0.9 copy-done.3
  2.2 2.6 %first.1 = bf16[128,32,256]{2,1,0:T(8,128)(2,1)S(1)} custom-call(bf16[16,256,128]{2,1,0:T(8,128)(2,1)S(1)} %copy-done.1, bf16[2,128,512]{2,1,0:T(8,128)(2,1)S(1)} %copy-done.3), custom_call_target="tpu_custom_call" | custom-call | tf_op jit(solution)/shard_map/first/pallas_call | solution.py:77
  4.8 1.3 copy-done
  6.1 16.4 %all-to-all-start = ((bf16[128,32,256]{2,1,0:T(8,128)(2,1)}), bf16[128,32,256]{2,1,0:T(8,128)(2,1)S(1)}, u32[]{:S(2)}, u32[]{:S(2)}) async-start(bf16[128,32,256]{2,1,0:T(8,128)(2,1)} %copy-done), calls=%async_computation | async-start | bytes 4194304 | tf_op jit(solution)/shard_map/all_to_all | solution.py:293
  22.4 0.0 copy-start.2
  22.5 48.2 %all-to-all-done = bf16[128,32,256]{2,1,0:T(8,128)(2,1)S(1)} async-done(((bf16[128,32,256]{2,1,0:T(8,128)(2,1)}), bf16[128,32,256]{2,1,0:T(8,128)(2,1)S(1)}, u32[]{:S(2)}, u32[]{:S(2)}) %all-to-all-start) | async-done | bytes 2097184 | tf_op jit(solution)/shard_map/all_to_all | solution.py:293
  70.7 0.7 other.1
  71.4 4.1 %collective-permute-start = (bf16[64,2,16,256]{3,2,1,0:T(8,128)(2,1)S(1)}, bf16[64,2,16,256]{3,2,1,0:T(8,128)(2,1)S(1)}, u32[]{:S(2)}, u32[]{:S(2)}) collective-permute-start(bf16[64,2,16,256]{3,2,1,0:T(8,128)(2,1)S(1)} %other.1), channel_id=1, source_target_pairs={{0,1},{1,0},{2,3},{3,2},{4,5},{5,4},{6,7},{7,6},{8,9},{9,8},{10,11... | collective-permute-start | bytes 3145736 | tf_op jit(solution)/shard_map/ppermute | solution.py:136
  75.5 1.5 own.1
  77.0 0.8 collective-permute-done.other_ref
  77.8 0.3 sum.1
  78.1 0.0 copy-start.4
  78.1 0.0 copy-start.6
  78.1 35.6 %all_to_all.20.tri_ref = bf16[128,16,256]{2,1,0:T(8,128)(2,1)S(1)} all-to-all(bf16[128,16,256]{2,1,0:T(8,128)(2,1)S(1)} %bitcast.11), channel_id=1, replica_groups=mesh['z'=8,'x'=4,'yl'=2,'yh'=2,'core'=2] {'z','x','yl','yh'}, dimensions={0} | all-to-all | bytes 2097152 | tf_op jit(solution)/shard_map/all_to_all | solution.py:293
  113.7 4.4 %middle.1 = (bf16[128,32,256]{2,1,0:T(8,128)(2,1)S(1)}, bf16[16,128,256]{2,1,0:T(8,128)(2,1)S(1)}) custom-call(bf16[128,16,256]{2,1,0:T(8,128)(2,1)S(1)} %all_to_all.20.tri_ref, bf16[16,128,256]{2,1,0:T(8,128)(2,1)S(1)} %get-tuple-element.13.z_ref, f32[16,128,256]{2,1,0:T(8,128)S(1)} %get-tuple-element.14.gate_ref, bf16[2,128,128]{2,1,0:T(8,128)(2,1)S(1)} %copy-done.6, ...), custom_call_target="tpu_custom_call" | custom-call | tf_op jit(solution)/shard_map/middle/pallas_call | solution.py:243
  118.2 55.8 %all_to_all.21 = bf16[128,32,256]{2,1,0:T(8,128)(2,1)S(1)} all-to-all(bf16[128,32,256]{2,1,0:T(8,128)(2,1)S(1)} %get-tuple-element.15), channel_id=1, replica_groups=mesh['z'=8,'x'=4,'yl'=2,'yh'=2,'core'=2] {'z','x','yl','yh'}, dimensions={0} | all-to-all | bytes 4194304 | tf_op jit(solution)/shard_map/all_to_all | solution.py:293
  174.0 0.1 slice.4
  174.1 5.1 %collective-permute-start.1 = (bf16[64,2,16,256]{3,2,1,0:T(8,128)(2,1)S(1)}, bf16[64,2,16,256]{3,2,1,0:T(8,128)(2,1)S(1)}, u32[]{:S(2)}, u32[]{:S(2)}) collective-permute-start(bf16[64,2,16,256]{3,2,1,0:T(8,128)(2,1)S(1)} %slice.4), channel_id=1, source_target_pairs={{0,1},{1,0},{2,3},{3,2},{4,5},{5,4},{6,7},{7,6},{8,9},{9,8},{10,11... | collective-permute-start | bytes 3145736 | tf_op jit(solution)/shard_map/ppermute | solution.py:198
  179.3 1.5 near.1
  180.8 0.7 collective-permute-done.1.left_ref
  181.6 0.8 far.1
  182.3 35.6 %all_to_all.22.tri_ref = bf16[128,16,256]{2,1,0:T(8,128)(2,1)S(1)} all-to-all(bf16[128,16,256]{2,1,0:T(8,128)(2,1)S(1)} %bitcast.10), channel_id=1, replica_groups=mesh['z'=8,'x'=4,'yl'=2,'yh'=2,'core'=2] {'z','x','yl','yh'}, dimensions={0} | all-to-all | bytes 2097152 | tf_op jit(solution)/shard_map/all_to_all | solution.py:293
  217.9 2.3 %last.1 = bf16[16,256,128]{2,1,0:T(8,128)(2,1)} custom-call(bf16[128,16,256]{2,1,0:T(8,128)(2,1)S(1)} %all_to_all.22.tri_ref, bf16[16,128,256]{2,1,0:T(8,128)(2,1)S(1)} %get-tuple-element.16.z_ref, f32[16,128,256]{2,1,0:T(8,128)S(1)} %get-tuple-element.18.gate_ref, bf16[2,128,128]{2,1,0:T(8,128)(2,1)S(1)} %copy-done.6), custom_call_target="tpu_custom_call" | custom-call | tf_op jit(solution)/shard_map/last/pallas_call | solution.py:276
  (8 shorter events, 0.0 us)
Async XLA Ops:
  0.0 1.2 copy-start.1
  1.2 0.9 copy-start.3
  4.8 1.3 copy-start
  6.1 64.6 %all-to-all-start = ((bf16[128,32,256]{2,1,0:T(8,128)(2,1)}), bf16[128,32,256]{2,1,0:T(8,128)(2,1)S(1)}, u32[]{:S(2)}, u32[]{:S(2)}) async-start(bf16[128,32,256]{2,1,0:T(8,128)(2,1)} %copy-done), calls=%async_computation | async-start | bytes 4194304 | tf_op jit(solution)/shard_map/all_to_all | solution.py:293
  22.4 53.1 %copy-start.2 = (bf16[16,256,128]{2,1,0:T(8,128)(2,1)S(1)}, bf16[16,256,128]{2,1,0:T(8,128)(2,1)}, u32[]{:S(2)}) copy-start(bf16[16,256,128]{2,1,0:T(8,128)(2,1)} %pair_ref.3) | copy-start | bytes 3145732
  22.5 53.1 %copy-start.5 = (bf16[2,128,128]{2,1,0:T(8,128)(2,1)S(1)}, bf16[2,128,128]{2,1,0:T(8,128)(2,1)}, u32[]{:S(2)}) copy-start(bf16[2,128,128]{2,1,0:T(8,128)(2,1)} %w_gate_ref.3) | copy-start | bytes 196612
  71.4 6.4 %collective-permute-start = (bf16[64,2,16,256]{3,2,1,0:T(8,128)(2,1)S(1)}, bf16[64,2,16,256]{3,2,1,0:T(8,128)(2,1)S(1)}, u32[]{:S(2)}, u32[]{:S(2)}) collective-permute-start(bf16[64,2,16,256]{3,2,1,0:T(8,128)(2,1)S(1)} %other.1), channel_id=1, source_target_pairs={{0,1},{1,0},{2,3},{3,2},{4,5},{5,4},{6,7},{7,6},{8,9},{9,8},{10,11... | collective-permute-start | bytes 3145736 | tf_op jit(solution)/shard_map/ppermute | solution.py:136
  78.1 35.6 %copy-start.4 = (bf16[2,128,512]{2,1,0:T(8,128)(2,1)S(1)}, bf16[2,128,512]{2,1,0:T(8,128)(2,1)}, u32[]{:S(2)}) copy-start(bf16[2,128,512]{2,1,0:T(8,128)(2,1)} %w_in_ref.3) | copy-start | bytes 786436
  78.1 35.6 %copy-start.6 = (bf16[2,128,128]{2,1,0:T(8,128)(2,1)S(1)}, bf16[2,128,128]{2,1,0:T(8,128)(2,1)}, u32[]{:S(2)}) copy-start(bf16[2,128,128]{2,1,0:T(8,128)(2,1)} %w_out_ref.3) | copy-start | bytes 196612
  174.1 7.4 %collective-permute-start.1 = (bf16[64,2,16,256]{3,2,1,0:T(8,128)(2,1)S(1)}, bf16[64,2,16,256]{3,2,1,0:T(8,128)(2,1)S(1)}, u32[]{:S(2)}, u32[]{:S(2)}) collective-permute-start(bf16[64,2,16,256]{3,2,1,0:T(8,128)(2,1)S(1)} %slice.4), channel_id=1, source_target_pairs={{0,1},{1,0},{2,3},{3,2},{4,5},{5,4},{6,7},{7,6},{8,9},{9,8},{10,11... | collective-permute-start | bytes 3145736 | tf_op jit(solution)/shard_map/ppermute | solution.py:198

commit v4 on v3

--- a/solution.py
+++ b/solution.py
@@ -63,29 +63,33 @@
             tri[:, c : c + 32, lane : lane + 128] = jnp.swapaxes(block, 0, 1)
 
 
-def first_kernel(pair_ref, w_in_ref, out_ref, sides, w_t):
+def first_kernel(core_ref, pair_ref, w_in_ref, out_ref, z_ref, sides, w_t):
     rows, _, hidden = pair_ref.shape
     w_t[...] = turned(w_in_ref[0])
     for r in range(rows):
-        x = norm(pair_ref[r].astype(F32).T).astype(BF16)
-        project(x, w_t[...], r, sides, hidden)
+        z = pair_ref[r].astype(F32).T
+        z_ref[r] = z.astype(BF16)
+        project(norm(z).astype(BF16), w_t[...], r, sides, hidden)
     by_channel(sides, out_ref)
 
 
-def first(pair, w_in):
+def first(core, pair, w_in):
     rows, cols, hidden = pair.shape
     return pl.pallas_call(
         first_kernel,
-        out_shape=jax.ShapeDtypeStruct((hidden, 2 * rows, cols), BF16),
-        in_specs=[VMEM, VMEM],
-        out_specs=VMEM,
+        out_shape=(
+            jax.ShapeDtypeStruct((hidden, 2 * rows, cols), BF16),
+            jax.ShapeDtypeStruct((rows, hidden, cols), BF16),
+        ),
+        in_specs=[SMEM, VMEM, VMEM],
+        out_specs=(VMEM, VMEM),
         scratch_shapes=[
             pltpu.VMEM((2, rows, hidden, cols), BF16),
             pltpu.VMEM((w_in.shape[2], hidden), BF16),
         ],
         compiler_params=params(),
         name="first",
-    )(pair, w_in)
+    )(core, pair, w_in)
 
 
 def products(got_ref, yo, core):
@@ -106,23 +110,21 @@
         out_ref[:, yo] = products(got_ref, yo, 1 - core_ref[0]).astype(BF16)
 
 
-def own_kernel(core_ref, got_ref, pair_ref, w_gate_ref, own_ref, z_ref, gate_ref, w_t):
+def own_kernel(core_ref, got_ref, z_ref, w_gate_ref, own_ref, gate_ref, w_t):
     for yo in range(2):
         own_ref[:, yo] = products(got_ref, yo, core_ref[0])
     w_t[...] = turned(w_gate_ref[0])
-    for r in range(pair_ref.shape[0]):
-        z = pair_ref[r].astype(F32).T
-        z_ref[r] = z.astype(BF16)
-        gate_ref[r] = sigmoid(dot(w_t[...], norm(z).astype(BF16)))
+    for r in range(z_ref.shape[0]):
+        gate_ref[r] = sigmoid(dot(w_t[...], norm(z_ref[r].astype(F32)).astype(BF16)))
 
 
 def sum_kernel(own_ref, other_ref, out_ref):
     out_ref[...] = (own_ref[...] + other_ref[...].astype(F32)).astype(BF16)
 
 
-def outgoing(got, core, pair, w_gate):
+def outgoing(got, core, z, w_gate):
     src, depth, cols = got.shape
-    rows, _, hidden = pair.shape
+    rows, hidden, _ = z.shape
     got = got.reshape(src // 2, 2, depth, cols)
     tri = (src // 2, 2, depth // 2, cols)
     other = pl.pallas_call(
@@ -134,19 +136,18 @@
         name="other",
     )(core, got)
     other = lax.ppermute(other, "core", [(0, 1), (1, 0)])
-    own, z, gates = pl.pallas_call(
+    own, gates = pl.pallas_call(
         own_kernel,
         out_shape=(
             jax.ShapeDtypeStruct(tri, F32),
-            jax.ShapeDtypeStruct((rows, hidden, cols), BF16),
             jax.ShapeDtypeStruct((rows, hidden, cols), F32),
         ),
         in_specs=[SMEM, VMEM, VMEM, VMEM],
-        out_specs=(VMEM,) * 3,
+        out_specs=(VMEM, VMEM),
         scratch_shapes=[pltpu.VMEM((hidden, hidden), BF16)],
         compiler_params=params(),
         name="own",
-    )(core, got, pair, w_gate)
+    )(core, got, z, w_gate)
     summed = pl.pallas_call(
         sum_kernel,
         out_shape=jax.ShapeDtypeStruct(tri, BF16),
@@ -155,7 +156,7 @@
         compiler_params=params(),
         name="sum",
     )(own, other)
-    return summed.reshape(src, depth // 2, cols), z, gates
+    return summed.reshape(src, depth // 2, cols), gates
 
 
 def columns(left, got_ref, yo):
@@ -295,8 +296,8 @@
 
 def on_device(pair, w_in, w_gate, w_out):
     core = lax.axis_index("core").reshape(1)
-    got = exchange(first(pair, w_in))
-    tri, z, gates = outgoing(got, core, pair, w_gate)
+    sent, z = first(core, pair, w_in)
+    tri, gates = outgoing(exchange(sent), core, z, w_gate)
     sent, z = middle(exchange(tri), z, gates, w_out, w_in)
     tri, gates = incoming(exchange(sent), core, z, w_gate)
     return last(exchange(tri), z, gates, w_out)

time: 222 us -> 221 us (level)
  blocking collectives: 127 us -> 191 us
  waiting for transfers between devices: 49.7 us -> 1.54 us
  starting transfers between devices: 25.6 us -> 9.24 us
    all_to_all x3 -> x4, blocking collectives: 127 us -> 191 us  [exchange(): lax.all_to_all(blocks, CHIPS, split_axis=0, concat_axis=0, tiled=True)]
    all_to_all x1 -> x0, waiting for transfers between devices: 48.2 us -> none  [exchange(): lax.all_to_all(blocks, CHIPS, split_axis=0, concat_axis=0, tiled=True)]
    all_to_all x1 -> x0, starting transfers between devices: 16.4 us -> none  [exchange(): lax.all_to_all(blocks, CHIPS, split_axis=0, concat_axis=0, tiled=True)]
  transfers between devices with their start and end apart: 3 -> 2, of which waited for: 3 -> 2; matrix products, arithmetic and copies ran while one was open for 0% -> 0% of each run, Pallas kernels for 1% -> 1%
where the time goes in v4:
time: 221 us; the launch traced here: 219 us
  blocking collectives  191 us (86%)
  Pallas kernels  14.1 us (6%)
  starting transfers between devices  9.24 us (4%)
  local copies, waits for them, and re-layouts  2.32 us (1%)
    all_to_all x4, blocking collectives, exchange(): lax.all_to_all(blocks, CHIPS, split_axis=0, concat_axis=0, tiled=True)  191 us
    ppermute x1, starting transfers between devices, incoming(): left = lax.ppermute(got[:, :, :depth // 2], 'core', [(0, 1), (1, 0)])  5.12 us
    pallas_call x1, Pallas kernels, middle(): pl.pallas_call(middle_kernel, out_shape=(jax.ShapeDtypeStruct((hidden, 2...  4.44 us
  transfers between devices with their start and end apart: 2, of which 2 were waited for; matrix products, arithmetic and copies ran while one was open for 0% of the time, Pallas kernels for 1%

profile of v4, /device:TPU:1, one launch (start us, length us, event | category | flops | bytes accessed | tf_op | source)
XLA Modules:
  0.0 218.8 jit_solution(7126343596853402646)
XLA Ops:
  0.0 0.9 copy-done
  1.0 1.2 copy-done.2
  2.2 2.6 %first.1 = (bf16[128,32,256]{2,1,0:T(8,128)(2,1)S(1)}, bf16[16,128,256]{2,1,0:T(8,128)(2,1)S(1)}) custom-call(s32[1]{0:T(128)} %bitcast.core_ref, bf16[16,256,128]{2,1,0:T(8,128)(2,1)S(1)} %copy-done.2, bf16[2,128,512]{2,1,0:T(8,128)(2,1)S(1)} %copy-done), custom_call_target="tpu_custom_call" | custom-call | tf_op jit(solution)/shard_map/first/pallas_call | solution.py:78
  4.8 64.3 %all_to_all.20 = bf16[128,32,256]{2,1,0:T(8,128)(2,1)S(1)} all-to-all(bf16[128,32,256]{2,1,0:T(8,128)(2,1)S(1)} %get-tuple-element.13), channel_id=1, replica_groups=mesh['z'=8,'x'=4,'yl'=2,'yh'=2,'core'=2] {'z','x','yl','yh'}, dimensions={0} | all-to-all | bytes 4194304 | tf_op jit(solution)/shard_map/all_to_all | solution.py:294
  69.1 0.7 other.1
  69.8 4.1 %collective-permute-start = (bf16[64,2,16,256]{3,2,1,0:T(8,128)(2,1)S(1)}, bf16[64,2,16,256]{3,2,1,0:T(8,128)(2,1)S(1)}, u32[]{:S(2)}, u32[]{:S(2)}) collective-permute-start(bf16[64,2,16,256]{3,2,1,0:T(8,128)(2,1)S(1)} %other.1), channel_id=1, source_target_pairs={{0,1},{1,0},{2,3},{3,2},{4,5},{5,4},{6,7},{7,6},{8,9},{9,8},{10,11... | collective-permute-start | bytes 3145736 | tf_op jit(solution)/shard_map/ppermute | solution.py:138
  74.0 0.0 copy-done.3
  74.0 1.5 own.1
  75.4 0.8 collective-permute-done.other_ref
  76.2 0.3 sum.1
  76.5 0.0 copy-start.1
  76.6 0.0 copy-start.4
  76.6 35.6 %all_to_all.21.tri_ref = bf16[128,16,256]{2,1,0:T(8,128)(2,1)S(1)} all-to-all(bf16[128,16,256]{2,1,0:T(8,128)(2,1)S(1)} %bitcast.11), channel_id=1, replica_groups=mesh['z'=8,'x'=4,'yl'=2,'yh'=2,'core'=2] {'z','x','yl','yh'}, dimensions={0} | all-to-all | bytes 2097152 | tf_op jit(solution)/shard_map/all_to_all | solution.py:294
  112.2 0.0 copy-done.1
  112.2 0.0 copy-done.4
  112.2 4.4 %middle.1 = (bf16[128,32,256]{2,1,0:T(8,128)(2,1)S(1)}, bf16[16,128,256]{2,1,0:T(8,128)(2,1)S(1)}) custom-call(bf16[128,16,256]{2,1,0:T(8,128)(2,1)S(1)} %all_to_all.21.tri_ref, bf16[16,128,256]{2,1,0:T(8,128)(2,1)S(1)} %get-tuple-element.14.z_ref, f32[16,128,256]{2,1,0:T(8,128)S(1)} %get-tuple-element.16.gate_ref, bf16[2,128,128]{2,1,0:T(8,128)(2,1)S(1)} %copy-done.4, ...), custom_call_target="tpu_custom_call" | custom-call | tf_op jit(solution)/shard_map/middle/pallas_call | solution.py:244
  116.6 55.8 %all_to_all.22 = bf16[128,32,256]{2,1,0:T(8,128)(2,1)S(1)} all-to-all(bf16[128,32,256]{2,1,0:T(8,128)(2,1)S(1)} %get-tuple-element.17), channel_id=1, replica_groups=mesh['z'=8,'x'=4,'yl'=2,'yh'=2,'core'=2] {'z','x','yl','yh'}, dimensions={0} | all-to-all | bytes 4194304 | tf_op jit(solution)/shard_map/all_to_all | solution.py:294
  172.5 0.1 slice.4
  172.6 5.1 %collective-permute-start.1 = (bf16[64,2,16,256]{3,2,1,0:T(8,128)(2,1)S(1)}, bf16[64,2,16,256]{3,2,1,0:T(8,128)(2,1)S(1)}, u32[]{:S(2)}, u32[]{:S(2)}) collective-permute-start(bf16[64,2,16,256]{3,2,1,0:T(8,128)(2,1)S(1)} %slice.4), channel_id=1, source_target_pairs={{0,1},{1,0},{2,3},{3,2},{4,5},{5,4},{6,7},{7,6},{8,9},{9,8},{10,11... | collective-permute-start | bytes 3145736 | tf_op jit(solution)/shard_map/ppermute | solution.py:199
  177.7 1.5 near.1
  179.3 0.7 collective-permute-done.1.left_ref
  180.0 0.8 far.1
  180.8 35.6 %all_to_all.23.tri_ref = bf16[128,16,256]{2,1,0:T(8,128)(2,1)S(1)} all-to-all(bf16[128,16,256]{2,1,0:T(8,128)(2,1)S(1)} %bitcast.10), channel_id=1, replica_groups=mesh['z'=8,'x'=4,'yl'=2,'yh'=2,'core'=2] {'z','x','yl','yh'}, dimensions={0} | all-to-all | bytes 2097152 | tf_op jit(solution)/shard_map/all_to_all | solution.py:294
  216.4 2.3 %last.1 = bf16[16,256,128]{2,1,0:T(8,128)(2,1)} custom-call(bf16[128,16,256]{2,1,0:T(8,128)(2,1)S(1)} %all_to_all.23.tri_ref, bf16[16,128,256]{2,1,0:T(8,128)(2,1)S(1)} %get-tuple-element.18.z_ref, f32[16,128,256]{2,1,0:T(8,128)S(1)} %get-tuple-element.20.gate_ref, bf16[2,128,128]{2,1,0:T(8,128)(2,1)S(1)} %copy-done.4), custom_call_target="tpu_custom_call" | custom-call | tf_op jit(solution)/shard_map/last/pallas_call | solution.py:277
  (3 shorter events, 0.0 us)
Async XLA Ops:
  0.0 0.9 copy-start
  1.0 1.2 copy-start.2
  69.1 4.9 %copy-start.3 = (bf16[2,128,128]{2,1,0:T(8,128)(2,1)S(1)}, bf16[2,128,128]{2,1,0:T(8,128)(2,1)}, u32[]{:S(2)}) copy-start(bf16[2,128,128]{2,1,0:T(8,128)(2,1)} %w_gate_ref.3) | copy-start | bytes 196612
  69.8 6.4 %collective-permute-start = (bf16[64,2,16,256]{3,2,1,0:T(8,128)(2,1)S(1)}, bf16[64,2,16,256]{3,2,1,0:T(8,128)(2,1)S(1)}, u32[]{:S(2)}, u32[]{:S(2)}) collective-permute-start(bf16[64,2,16,256]{3,2,1,0:T(8,128)(2,1)S(1)} %other.1), channel_id=1, source_target_pairs={{0,1},{1,0},{2,3},{3,2},{4,5},{5,4},{6,7},{7,6},{8,9},{9,8},{10,11... | collective-permute-start | bytes 3145736 | tf_op jit(solution)/shard_map/ppermute | solution.py:138
  76.5 35.6 %copy-start.1 = (bf16[2,128,512]{2,1,0:T(8,128)(2,1)S(1)}, bf16[2,128,512]{2,1,0:T(8,128)(2,1)}, u32[]{:S(2)}) copy-start(bf16[2,128,512]{2,1,0:T(8,128)(2,1)} %w_in_ref.3) | copy-start | bytes 786436
  76.6 35.6 %copy-start.4 = (bf16[2,128,128]{2,1,0:T(8,128)(2,1)S(1)}, bf16[2,128,128]{2,1,0:T(8,128)(2,1)}, u32[]{:S(2)}) copy-start(bf16[2,128,128]{2,1,0:T(8,128)(2,1)} %w_out_ref.3) | copy-start | bytes 196612
  172.6 7.4 %collective-permute-start.1 = (bf16[64,2,16,256]{3,2,1,0:T(8,128)(2,1)S(1)}, bf16[64,2,16,256]{3,2,1,0:T(8,128)(2,1)S(1)}, u32[]{:S(2)}, u32[]{:S(2)}) collective-permute-start(bf16[64,2,16,256]{3,2,1,0:T(8,128)(2,1)S(1)} %slice.4), channel_id=1, source_target_pairs={{0,1},{1,0},{2,3},{3,2},{4,5},{5,4},{6,7},{7,6},{8,9},{9,8},{10,11... | collective-permute-start | bytes 3145736 | tf_op jit(solution)/shard_map/ppermute | solution.py:199

commit v5 on v4

--- a/solution.py
+++ b/solution.py
@@ -14,7 +14,7 @@
 
 
 def params():
-    return pltpu.CompilerParams(vmem_limit_bytes=24 * 1024 * 1024)
+    return pltpu.CompilerParams(vmem_limit_bytes=14 * 1024 * 1024)
 
 
 def sigmoid(v):
@@ -55,12 +55,13 @@
                 )
 
 
-def by_row(tri_ref, tri):
-    hidden, _, cols = tri_ref.shape
-    for lane in range(0, cols, 128):
-        for c in range(0, hidden, 32):
-            block = tri_ref[c : c + 32, :, lane : lane + 128]
-            tri[:, c : c + 32, lane : lane + 128] = jnp.swapaxes(block, 0, 1)
+def by_row(tri_refs, tri):
+    for at, tri_ref in enumerate(tri_refs):
+        hidden, _, cols = tri_ref.shape
+        for lane in range(0, cols, 128):
+            for c in range(0, hidden, 32):
+                block = tri_ref[c : c + 32, :, lane : lane + 128]
+                tri[:, c : c + 32, at * cols + lane : at * cols + lane + 128] = jnp.swapaxes(block, 0, 1)
 
 
 def first_kernel(core_ref, pair_ref, w_in_ref, out_ref, z_ref, sides, w_t):
@@ -110,21 +111,20 @@
         out_ref[:, yo] = products(got_ref, yo, 1 - core_ref[0]).astype(BF16)
 
 
-def own_kernel(core_ref, got_ref, z_ref, w_gate_ref, own_ref, gate_ref, w_t):
+def own_kernel(core_ref, got_ref, own_ref):
     for yo in range(2):
         own_ref[:, yo] = products(got_ref, yo, core_ref[0])
-    w_t[...] = turned(w_gate_ref[0])
-    for r in range(z_ref.shape[0]):
-        gate_ref[r] = sigmoid(dot(w_t[...], norm(z_ref[r].astype(F32)).astype(BF16)))
-
-
-def sum_kernel(own_ref, other_ref, out_ref):
-    out_ref[...] = (own_ref[...] + other_ref[...].astype(F32)).astype(BF16)
-
-
-def outgoing(got, core, z, w_gate):
+
+
+def sum_kernel(own_ref, other_ref, *out_refs):
+    for at, out_ref in enumerate(out_refs):
+        lanes = pl.ds(at * 128, 128)
+        summed = own_ref[:, :, :, lanes] + other_ref[:, :, :, lanes].astype(F32)
+        out_ref[...] = summed.astype(BF16)
+
+
+def outgoing(got, core):
     src, depth, cols = got.shape
-    rows, hidden, _ = z.shape
     got = got.reshape(src // 2, 2, depth, cols)
     tri = (src // 2, 2, depth // 2, cols)
     other = pl.pallas_call(
@@ -136,27 +136,23 @@
         name="other",
     )(core, got)
     other = lax.ppermute(other, "core", [(0, 1), (1, 0)])
-    own, gates = pl.pallas_call(
+    own = pl.pallas_call(
         own_kernel,
-        out_shape=(
-            jax.ShapeDtypeStruct(tri, F32),
-            jax.ShapeDtypeStruct((rows, hidden, cols), F32),
-        ),
-        in_specs=[SMEM, VMEM, VMEM, VMEM],
-        out_specs=(VMEM, VMEM),
-        scratch_shapes=[pltpu.VMEM((hidden, hidden), BF16)],
+        out_shape=jax.ShapeDtypeStruct(tri, F32),
+        in_specs=[SMEM, VMEM],
+        out_specs=VMEM,
         compiler_params=params(),
         name="own",
-    )(core, got, z, w_gate)
+    )(core, got)
     summed = pl.pallas_call(
         sum_kernel,
-        out_shape=jax.ShapeDtypeStruct(tri, BF16),
+        out_shape=[jax.ShapeDtypeStruct(tri[:3] + (128,), BF16)] * (cols // 128),
         in_specs=[VMEM, VMEM],
-        out_specs=VMEM,
+        out_specs=[VMEM] * (cols // 128),
         compiler_params=params(),
         name="sum",
     )(own, other)
-    return summed.reshape(src, depth // 2, cols), gates
+    return [half.reshape(src, depth // 2, 128) for half in summed]
 
 
 def columns(left, got_ref, yo):
@@ -220,52 +216,55 @@
     return out.reshape(src, depth // 2, cols), gates
 
 
-def updated(tri, z_ref, gate_ref, w_out_t, r):
+def updated(tri, z_ref, gates, w_out_t, r):
     y = norm(tri[r].astype(F32)).astype(BF16)
-    return z_ref[r].astype(F32) + gate_ref[r] * dot(w_out_t[...], y)
+    return z_ref[r].astype(F32) + gates * dot(w_out_t[...], y)
 
 
 def middle_kernel(
-    tri_ref, z_ref, gate_ref, w_out_ref, w_in_ref, out_ref, z_new_ref, tri, sides, w_out_t, w_in_t
+    a_ref, b_ref, z_ref, w_gate_ref, w_out_ref, w_in_ref, out_ref, z_new_ref, tri, sides, w_out_t, w_in_t, w_gate_t
 ):
-    hidden, rows, _ = tri_ref.shape
+    hidden, rows, _ = a_ref.shape
     w_out_t[...] = turned(w_out_ref[0])
     w_in_t[...] = turned(w_in_ref[1])
-    by_row(tri_ref, tri)
+    w_gate_t[...] = turned(w_gate_ref[0])
+    by_row([a_ref, b_ref], tri)
     for r in range(rows):
-        z = updated(tri, z_ref, gate_ref, w_out_t, r).astype(BF16)
+        gates = sigmoid(dot(w_gate_t[...], norm(z_ref[r].astype(F32)).astype(BF16)))
+        z = updated(tri, z_ref, gates, w_out_t, r).astype(BF16)
         z_new_ref[r] = z
         project(norm(z.astype(F32)).astype(BF16), w_in_t[...], r, sides, hidden)
     by_channel(sides, out_ref)
 
 
-def middle(tri, z, gates, w_out, w_in):
-    hidden, rows, cols = tri.shape
+def middle(halves, z, w_gate, w_out, w_in):
+    rows, hidden, cols = z.shape
     return pl.pallas_call(
         middle_kernel,
         out_shape=(
             jax.ShapeDtypeStruct((hidden, 2 * rows, cols), BF16),
             jax.ShapeDtypeStruct((rows, hidden, cols), BF16),
         ),
-        in_specs=[VMEM] * 5,
+        in_specs=[VMEM] * 6,
         out_specs=(VMEM, VMEM),
         scratch_shapes=[
             pltpu.VMEM((rows, hidden, cols), BF16),
             pltpu.VMEM((2, rows, hidden, cols), BF16),
             pltpu.VMEM((hidden, hidden), BF16),
             pltpu.VMEM((w_in.shape[2], hidden), BF16),
+            pltpu.VMEM((hidden, hidden), BF16),
         ],
         compiler_params=params(),
         name="middle",
-    )(tri, z, gates, w_out, w_in)
+    )(*halves, z, w_gate, w_out, w_in)
 
 
 def last_kernel(tri_ref, z_ref, gate_ref, w_out_ref, out_ref, tri, rows_out, w_out_t, sems):
     w_out_t[...] = turned(w_out_ref[1])
-    by_row(tri_ref, tri)
+    by_row([tri_ref], tri)
     copies = []
     for r in range(tri_ref.shape[1]):
-        rows_out[r] = updated(tri, z_ref, gate_ref, w_out_t, r).T.astype(BF16)
+        rows_out[r] = updated(tri, z_ref, gate_ref[r], w_out_t, r).T.astype(BF16)
         copies.append(pltpu.make_async_copy(rows_out.at[r], out_ref.at[r], sems.at[r]))
         copies[-1].start()
     for copy in copies:
@@ -294,11 +293,29 @@
     return lax.all_to_all(blocks, CHIPS, split_axis=0, concat_axis=0, tiled=True)
 
 
+def plane_first(a, b):
+    both = jnp.concatenate([a, b], axis=2)
+    shape = both.shape
+    planes = 8
+    both = both.reshape(planes, -1, *shape[1:]).swapaxes(0, 1)
+    both = lax.all_to_all(both, CHIPS[1:], split_axis=0, concat_axis=0, tiled=True)
+    both = both.swapaxes(0, 1)
+    both = lax.all_to_all(both, CHIPS[0], split_axis=0, concat_axis=0, tiled=True)
+    both = both.reshape(shape)
+    return both[:, :, :128], both[:, :, 128:]
+
+
+def at_once(a, b):
+    both = exchange(jnp.concatenate([a, b], axis=2))
+    return both[:, :, :128], both[:, :, 128:]
+
+
 def on_device(pair, w_in, w_gate, w_out):
     core = lax.axis_index("core").reshape(1)
     sent, z = first(core, pair, w_in)
-    tri, gates = outgoing(exchange(sent), core, z, w_gate)
-    sent, z = middle(exchange(tri), z, gates, w_out, w_in)
+    tri = outgoing(exchange(sent), core)
+    tri = lax.cond(core[0] == 0, at_once, plane_first, *tri)
+    sent, z = middle(tri, z, w_gate, w_out, w_in)
     tri, gates = incoming(exchange(sent), core, z, w_gate)
     return last(exchange(tri), z, gates, w_out)
 

time: 221 us -> 217 us (0.982)
  starting transfers between devices: 9.24 us -> 4.13 us
    all_to_all x4 -> x3, blocking collectives: 191 us -> 152 us  [exchange(): lax.all_to_all(blocks, CHIPS, split_axis=0, concat_axis=0, tiled=True)]
    all_to_all x0 -> x2, blocking collectives: none -> 38.1 us  [the longest x1 20.5 us: plane_first(): lax.all_to_all(both, CHIPS[0], split_axis=0, concat_axis=0, tiled=True)]
    ppermute x1, starting transfers between devices: 5.12 us -> 0.09 us  [incoming(): left = lax.ppermute(got[:, :, :depth // 2], 'core', [(0, 1), (1, 0)])]
where the time goes in v5:
time: 217 us; the launch traced here: 215 us
  blocking collectives  190 us (88%)
  Pallas kernels  14.8 us (7%)
  starting transfers between devices  4.13 us (2%)
  waiting for transfers between devices  2.85 us (1%)
  local copies, waits for them, and re-layouts  2.68 us (1%)
    all_to_all x3, blocking collectives, exchange(): lax.all_to_all(blocks, CHIPS, split_axis=0, concat_axis=0, tiled=True)  152 us
    all_to_all x1, blocking collectives, plane_first(): lax.all_to_all(both, CHIPS[0], split_axis=0, concat_axis=0, tiled=True)  20.5 us
    all_to_all x1, blocking collectives, plane_first(): lax.all_to_all(both, CHIPS[1:], split_axis=0, concat_axis=0, tiled=True)  17.6 us
    pallas_call x1, Pallas kernels, middle(): pl.pallas_call(middle_kernel, out_shape=(jax.ShapeDtypeStruct((hidden, 2...  4.91 us
  transfers between devices with their start and end apart: 2, of which 2 were waited for; matrix products, arithmetic and copies ran while one was open for 0% of the time, Pallas kernels for 1%

profile of v5, /device:TPU:1, one launch (start us, length us, event | category | flops | bytes accessed | tf_op | source)
XLA Modules:
  0.0 215.4 jit_solution(1025929763304388099)
XLA Ops:
  0.0 0.9 copy-done
  1.0 1.2 copy-done.2
  2.2 2.6 %first.1 = (bf16[128,32,256]{2,1,0:T(8,128)(2,1)S(1)}, bf16[16,128,256]{2,1,0:T(8,128)(2,1)S(1)}) custom-call(s32[1]{0:T(128)} %bitcast.5.core_ref, bf16[16,256,128]{2,1,0:T(8,128)(2,1)S(1)} %copy-done.2, bf16[2,128,512]{2,1,0:T(8,128)(2,1)S(1)} %copy-done), custom_call_target="tpu_custom_call" | custom-call | tf_op jit(solution)/shard_map/first/pallas_call | solution.py:79
  4.8 64.3 %all_to_all.30 = bf16[128,32,256]{2,1,0:T(8,128)(2,1)S(1)} all-to-all(bf16[128,32,256]{2,1,0:T(8,128)(2,1)S(1)} %get-tuple-element.27), channel_id=1, replica_groups=mesh['z'=8,'x'=4,'yl'=2,'yh'=2,'core'=2] {'z','x','yl','yh'}, dimensions={0} | all-to-all | bytes 4194304 | tf_op jit(solution)/shard_map/all_to_all | solution.py:293
  69.1 1.7 other.1
  70.8 4.0 %collective-permute-start = (bf16[64,2,16,256]{3,2,1,0:T(8,128)(2,1)}, bf16[64,2,16,256]{3,2,1,0:T(8,128)(2,1)S(1)}, u32[]{:S(2)}, u32[]{:S(2)}) collective-permute-start(bf16[64,2,16,256]{3,2,1,0:T(8,128)(2,1)} %other.1), channel_id=1, source_target_pairs={{0,1},{1,0},{2,3},{3,2},{4,5},{5,4},{6,7},{7,6},{8,9},{9,8},{10,11... | collective-permute-start | bytes 3145736 | tf_op jit(solution)/shard_map/ppermute | solution.py:138
  74.9 0.7 own.1.own_ref
  75.6 1.8 collective-permute-done.other_ref
  77.3 0.2 sum.1
  77.6 38.8 %conditional.1 = (bf16[128,16,128]{2,1,0:T(8,128)(2,1)S(1)}, bf16[128,16,128]{2,1,0:T(8,128)(2,1)S(1)}) conditional(s32[]{:T(128)} %convert_element_type.3, (bf16[128,16,128]{2,1,0:T(8,128)(2,1)S(1)}, bf16[128,16,128]{2,1,0:T(8,128)(2,1)S(1)}) %tuple.20, (bf16[128,16,128]{2,1,0:T(8,128)(2,1)S(1)}, bf16[128,16,128]{2,1,0:T(8,128)(2,1)S(1)}) %tuple.21), branch_computations={%region_0.0_spmd, %region_1.0_spmd} | conditional | flops 2097152 | bytes 12582928 | solution.py:317
  77.6 0.1 pad_maximum_fusion
  77.7 0.1 copy.5
  77.9 17.6 %all_to_all.27 = bf16[16,8,16,256]{3,2,1,0:T(8,128)(2,1)S(1)} all-to-all(bf16[16,8,16,256]{3,2,1,0:T(8,128)(2,1)S(1)} %copy.5), channel_id=1, replica_groups=mesh['z'=8,'x'=4,'yl'=2,'yh'=2,'core'=2] {'x','yl','yh'}, dimensions={0} | all-to-all | bytes 2097152 | tf_op jit(solution)/shard_map/cond/branch_0_fun/all_to_all | solution.py:301
  95.5 20.5 %all_to_all.28 = bf16[8,16,16,256]{3,2,1,0:T(8,128)(2,1)S(1)} all-to-all(bf16[8,16,16,256]{3,2,1,0:T(8,128)(2,1)S(1)} %bitcast.20), channel_id=1, replica_groups=mesh['z'=8,'x'=4,'yl'=2,'yh'=2,'core'=2] {'z'}, dimensions={0} | all-to-all | bytes 2097152 | tf_op jit(solution)/shard_map/cond/branch_0_fun/all_to_all | solution.py:303
  116.1 0.2 fusion
  116.5 4.9 %middle.1 = (bf16[128,32,256]{2,1,0:T(8,128)(2,1)S(1)}, bf16[16,128,256]{2,1,0:T(8,128)(2,1)S(1)}) custom-call(bf16[128,16,128]{2,1,0:T(8,128)(2,1)S(1)} %get-tuple-element.30.a_ref, bf16[128,16,128]{2,1,0:T(8,128)(2,1)S(1)} %get-tuple-element.31.b_ref, bf16[16,128,256]{2,1,0:T(8,128)(2,1)S(1)} %copy-done.4, bf16[2,128,128]{2,1,0:T(8,128)(2,1)S(1)} %copy-done.5, ...), custom_call_target="tpu_custom_call" | custom-call | tf_op jit(solution)/shard_map/middle/pallas_call | solution.py:242
  121.4 52.0 %all_to_all.31 = bf16[128,32,256]{2,1,0:T(8,128)(2,1)S(1)} all-to-all(bf16[128,32,256]{2,1,0:T(8,128)(2,1)S(1)} %get-tuple-element.33), channel_id=1, replica_groups=mesh['z'=8,'x'=4,'yl'=2,'yh'=2,'core'=2] {'z','x','yl','yh'}, dimensions={0} | all-to-all | bytes 4194304 | tf_op jit(solution)/shard_map/all_to_all | solution.py:293
  173.4 0.1 slice.20
  173.5 0.1 collective-permute-start.1
  173.6 1.5 near.1
  175.2 1.1 collective-permute-done.1.left_ref
  176.3 0.8 far.1
  177.1 35.9 %all_to_all.32.tri_ref = bf16[128,16,256]{2,1,0:T(8,128)(2,1)S(1)} all-to-all(bf16[128,16,256]{2,1,0:T(8,128)(2,1)S(1)} %bitcast.18), channel_id=1, replica_groups=mesh['z'=8,'x'=4,'yl'=2,'yh'=2,'core'=2] {'z','x','yl','yh'}, dimensions={0} | all-to-all | bytes 2097152 | tf_op jit(solution)/shard_map/all_to_all | solution.py:293
  213.0 2.3 %last.1 = bf16[16,256,128]{2,1,0:T(8,128)(2,1)} custom-call(bf16[128,16,256]{2,1,0:T(8,128)(2,1)S(1)} %all_to_all.32.tri_ref, bf16[16,128,256]{2,1,0:T(8,128)(2,1)S(1)} %get-tuple-element.34.z_ref, f32[16,128,256]{2,1,0:T(8,128)S(1)} %get-tuple-element.36.gate_ref, bf16[2,128,128]{2,1,0:T(8,128)(2,1)S(1)} %copy-done.6), custom_call_target="tpu_custom_call" | custom-call | tf_op jit(solution)/shard_map/last/pallas_call | solution.py:276
  (13 shorter events, 0.1 us)
Async XLA Ops:
  0.0 0.9 copy-start
  1.0 1.2 copy-start.2
  4.8 64.4 %copy-start.3 = (bf16[16,128,256]{2,1,0:T(8,128)(2,1)}, bf16[16,128,256]{2,1,0:T(8,128)(2,1)S(1)}, u32[]{:S(2)}) copy-start(bf16[16,128,256]{2,1,0:T(8,128)(2,1)S(1)} %get-tuple-element.32.z_ref) | copy-start | bytes 3145732
  70.8 6.5 %collective-permute-start = (bf16[64,2,16,256]{3,2,1,0:T(8,128)(2,1)}, bf16[64,2,16,256]{3,2,1,0:T(8,128)(2,1)S(1)}, u32[]{:S(2)}, u32[]{:S(2)}) collective-permute-start(bf16[64,2,16,256]{3,2,1,0:T(8,128)(2,1)} %other.1), channel_id=1, source_target_pairs={{0,1},{1,0},{2,3},{3,2},{4,5},{5,4},{6,7},{7,6},{8,9},{9,8},{10,11... | collective-permute-start | bytes 3145736 | tf_op jit(solution)/shard_map/ppermute | solution.py:138
  77.6 38.9 %copy-start.1 = (bf16[2,128,512]{2,1,0:T(8,128)(2,1)S(1)}, bf16[2,128,512]{2,1,0:T(8,128)(2,1)}, u32[]{:S(2)}) copy-start(bf16[2,128,512]{2,1,0:T(8,128)(2,1)} %w_in_ref.3) | copy-start | bytes 786436
  77.6 38.9 %copy-start.4 = (bf16[16,128,256]{2,1,0:T(8,128)(2,1)S(1)}, bf16[16,128,256]{2,1,0:T(8,128)(2,1)}, u32[]{:S(2)}) copy-start(bf16[16,128,256]{2,1,0:T(8,128)(2,1)} %copy-done.3) | copy-start | bytes 3145732
  77.6 38.9 %copy-start.5 = (bf16[2,128,128]{2,1,0:T(8,128)(2,1)S(1)}, bf16[2,128,128]{2,1,0:T(8,128)(2,1)}, u32[]{:S(2)}) copy-start(bf16[2,128,128]{2,1,0:T(8,128)(2,1)} %w_gate_ref.3) | copy-start | bytes 196612
  77.6 38.9 %copy-start.6 = (bf16[2,128,128]{2,1,0:T(8,128)(2,1)S(1)}, bf16[2,128,128]{2,1,0:T(8,128)(2,1)}, u32[]{:S(2)}) copy-start(bf16[2,128,128]{2,1,0:T(8,128)(2,1)} %w_out_ref.3) | copy-start | bytes 196612
  173.5 2.7 %collective-permute-start.1 = (bf16[64,2,16,256]{3,2,1,0:T(8,128)(2,1)S(1)}, bf16[64,2,16,256]{3,2,1,0:T(8,128)(2,1)S(1)}, u32[]{:S(2)}, u32[]{:S(2)}) collective-permute-start(bf16[64,2,16,256]{3,2,1,0:T(8,128)(2,1)S(1)} %slice.20), channel_id=1, source_target_pairs={{0,1},{1,0},{2,3},{3,2},{4,5},{5,4},{6,7},{7,6},{8,9},{9,8},{10,11... | collective-permute-start | bytes 3145736 | tf_op jit(solution)/shard_map/ppermute | solution.py:195

commit v6 on v5

--- a/solution.py
+++ b/solution.py
@@ -293,16 +293,17 @@
     return lax.all_to_all(blocks, CHIPS, split_axis=0, concat_axis=0, tiled=True)
 
 
-def plane_first(a, b):
-    both = jnp.concatenate([a, b], axis=2)
-    shape = both.shape
-    planes = 8
-    both = both.reshape(planes, -1, *shape[1:]).swapaxes(0, 1)
-    both = lax.all_to_all(both, CHIPS[1:], split_axis=0, concat_axis=0, tiled=True)
-    both = both.swapaxes(0, 1)
-    both = lax.all_to_all(both, CHIPS[0], split_axis=0, concat_axis=0, tiled=True)
-    both = both.reshape(shape)
-    return both[:, :, :128], both[:, :, 128:]
+def along(blocks, first, second):
+    shape = blocks.shape
+    blocks = blocks.reshape(lax.axis_size(CHIPS[0]), -1, *shape[1:])
+    for axes in (first, second):
+        if axes == CHIPS[0]:
+            blocks = lax.all_to_all(blocks, axes, split_axis=0, concat_axis=0, tiled=True)
+        else:
+            blocks = blocks.swapaxes(0, 1)
+            blocks = lax.all_to_all(blocks, axes, split_axis=0, concat_axis=0, tiled=True)
+            blocks = blocks.swapaxes(0, 1)
+    return blocks.reshape(shape)
 
 
 def at_once(a, b):
@@ -310,10 +311,19 @@
     return both[:, :, :128], both[:, :, 128:]
 
 
+def plane_first(a, b):
+    both = along(jnp.concatenate([a, b], axis=2), CHIPS[1:], CHIPS[0])
+    return both[:, :, :128], both[:, :, 128:]
+
+
+def plane_then_z(blocks):
+    return along(blocks, CHIPS[1:], CHIPS[0])
+
+
 def on_device(pair, w_in, w_gate, w_out):
     core = lax.axis_index("core").reshape(1)
     sent, z = first(core, pair, w_in)
-    tri = outgoing(exchange(sent), core)
+    tri = outgoing(lax.cond(core[0] == 0, exchange, plane_then_z, sent), core)
     tri = lax.cond(core[0] == 0, at_once, plane_first, *tri)
     sent, z = middle(tri, z, w_gate, w_out, w_in)
     tri, gates = incoming(exchange(sent), core, z, w_gate)

time: 217 us -> 214 us (0.986)
  starting transfers between devices: 4.13 us -> 0.19 us
    all_to_all x2 -> x4, blocking collectives: 38.1 us -> 108 us  [along(): lax.all_to_all(blocks, axes, split_axis=0, concat_axis=0, tiled=True)]
    all_to_all x3 -> x2, blocking collectives: 152 us -> 83.5 us  [exchange(): lax.all_to_all(blocks, CHIPS, split_axis=0, concat_axis=0, tiled=True)]
    ppermute x1, starting transfers between devices: 4.03 us -> 0.09 us  [outgoing(): other = lax.ppermute(other, 'core', [(0, 1), (1, 0)])]
where the time goes in v6:
time: 214 us; the launch traced here: 212 us
  blocking collectives  191 us (89%)
  Pallas kernels  13.8 us (6%)
  local copies, waits for them, and re-layouts  3.14 us (1%)
  waiting for transfers between devices  3 us (1%)
    all_to_all x4, blocking collectives, along(): lax.all_to_all(blocks, axes, split_axis=0, concat_axis=0, tiled=True)  108 us
    all_to_all x2, blocking collectives, exchange(): lax.all_to_all(blocks, CHIPS, split_axis=0, concat_axis=0, tiled=True)  83.5 us
    pallas_call x1, Pallas kernels, middle(): pl.pallas_call(middle_kernel, out_shape=(jax.ShapeDtypeStruct((hidden, 2...  4.91 us
  transfers between devices with their start and end apart: 2, of which 2 were waited for; matrix products, arithmetic and copies ran while one was open for 0% of the time, Pallas kernels for 1%

profile of v6, /device:TPU:1, one launch (start us, length us, event | category | flops | bytes accessed | tf_op | source)
XLA Modules:
  0.0 211.9 jit_solution(11915486195131334583)
XLA Ops:
  0.0 0.9 copy-done
  1.0 1.2 copy-done.2
  2.2 2.6 %first.1 = (bf16[128,32,256]{2,1,0:T(8,128)(2,1)S(1)}, bf16[16,128,256]{2,1,0:T(8,128)(2,1)S(1)}) custom-call(s32[1]{0:T(128)} %bitcast.11.core_ref, bf16[16,256,128]{2,1,0:T(8,128)(2,1)S(1)} %copy-done.2, bf16[2,128,512]{2,1,0:T(8,128)(2,1)S(1)} %copy-done), custom_call_target="tpu_custom_call" | custom-call | tf_op jit(solution)/shard_map/first/pallas_call | solution.py:79
  4.7 67.7 %conditional.2 = (bf16[64,2,32,256]{3,2,1,0:T(8,128)(2,1)S(1)}) conditional(s32[]{:T(128)} %convert_element_type.4, bf16[128,32,256]{2,1,0:T(8,128)(2,1)S(1)} %get-tuple-element.33, bf16[128,32,256]{2,1,0:T(8,128)(2,1)S(1)} %get-tuple-element.33), branch_computations={%region_0.0_spmd, %region_1.0_spmd} | conditional | bytes 16777224 | solution.py:326
  4.8 0.2 copy.5
  5.0 27.7 %all_to_all.34 = bf16[16,8,32,256]{3,2,1,0:T(8,128)(2,1)S(1)} all-to-all(bf16[16,8,32,256]{3,2,1,0:T(8,128)(2,1)S(1)} %copy.5), channel_id=1, replica_groups=mesh['z'=8,'x'=4,'yl'=2,'yh'=2,'core'=2] {'x','yl','yh'}, dimensions={0} | all-to-all | bytes 4194304 | tf_op jit(solution)/shard_map/cond/branch_0_fun/all_to_all | solution.py:304
  32.7 0.2 copy.11
  32.9 39.6 %all_to_all.35 = bf16[8,16,32,256]{3,2,1,0:T(8,128)(2,1)S(1)} all-to-all(bf16[8,16,32,256]{3,2,1,0:T(8,128)(2,1)S(1)} %bitcast.27), channel_id=1, replica_groups=mesh['z'=8,'x'=4,'yl'=2,'yh'=2,'core'=2] {'z'}, dimensions={0} | all-to-all | bytes 4194304 | tf_op jit(solution)/shard_map/cond/branch_0_fun/all_to_all | solution.py:301
  72.5 0.7 other.1
  73.3 0.7 own.1.own_ref
  74.1 1.9 collective-permute-done.other_ref
  76.0 0.3 sum.1
  76.3 41.0 %conditional.3 = (bf16[128,16,128]{2,1,0:T(8,128)(2,1)S(1)}, bf16[128,16,128]{2,1,0:T(8,128)(2,1)S(1)}) conditional(s32[]{:T(128)} %convert_element_type.4, (bf16[128,16,128]{2,1,0:T(8,128)(2,1)S(1)}, bf16[128,16,128]{2,1,0:T(8,128)(2,1)S(1)}) %tuple.30, (bf16[128,16,128]{2,1,0:T(8,128)(2,1)S(1)}, bf16[128,16,128]{2,1,0:T(8,128)(2,1)S(1)}) %tuple.31), branch_computations={%region_2.0_spmd, %region_3.0_spmd} | conditional | flops 2097152 | bytes 12582928 | solution.py:327
  76.3 0.1 pad_maximum_fusion
  76.5 20.1 %all_to_all.37 = bf16[16,8,16,256]{3,2,1,0:T(8,128)(2,1)S(1)} all-to-all(bf16[16,8,16,256]{3,2,1,0:T(8,128)(2,1)S(1)} %copy.7), channel_id=1, replica_groups=mesh['z'=8,'x'=4,'yl'=2,'yh'=2,'core'=2] {'x','yl','yh'}, dimensions={0} | all-to-all | bytes 2097152 | tf_op jit(solution)/shard_map/cond/branch_0_fun/all_to_all | solution.py:304
  96.8 20.2 %all_to_all.38 = bf16[8,16,16,256]{3,2,1,0:T(8,128)(2,1)S(1)} all-to-all(bf16[8,16,16,256]{3,2,1,0:T(8,128)(2,1)S(1)} %bitcast.29), channel_id=1, replica_groups=mesh['z'=8,'x'=4,'yl'=2,'yh'=2,'core'=2] {'z'}, dimensions={0} | all-to-all | bytes 2097152 | tf_op jit(solution)/shard_map/cond/branch_0_fun/all_to_all | solution.py:301
  116.9 0.2 fusion
  117.3 4.9 %middle.1 = (bf16[128,32,256]{2,1,0:T(8,128)(2,1)S(1)}, bf16[16,128,256]{2,1,0:T(8,128)(2,1)S(1)}) custom-call(bf16[128,16,128]{2,1,0:T(8,128)(2,1)S(1)} %get-tuple-element.36.a_ref, bf16[128,16,128]{2,1,0:T(8,128)(2,1)S(1)} %get-tuple-element.37.b_ref, bf16[16,128,256]{2,1,0:T(8,128)(2,1)S(1)} %get-tuple-element.38.z_ref, ...), custom_call_target="tpu_custom_call" | custom-call | tf_op jit(solution)/shard_map/middle/pallas_call | solution.py:242
  122.3 47.6 %all_to_all.40 = bf16[128,32,256]{2,1,0:T(8,128)(2,1)S(1)} all-to-all(bf16[128,32,256]{2,1,0:T(8,128)(2,1)S(1)} %get-tuple-element.39), channel_id=1, replica_groups=mesh['z'=8,'x'=4,'yl'=2,'yh'=2,'core'=2] {'z','x','yl','yh'}, dimensions={0} | all-to-all | bytes 4194304 | tf_op jit(solution)/shard_map/all_to_all | solution.py:293
  170.1 1.5 near.1
  171.6 1.1 collective-permute-done.1.left_ref
  172.7 0.8 far.1
  173.5 35.9 %all_to_all.41.tri_ref = bf16[128,16,256]{2,1,0:T(8,128)(2,1)S(1)} all-to-all(bf16[128,16,256]{2,1,0:T(8,128)(2,1)S(1)} %bitcast.23), channel_id=1, replica_groups=mesh['z'=8,'x'=4,'yl'=2,'yh'=2,'core'=2] {'z','x','yl','yh'}, dimensions={0} | all-to-all | bytes 2097152 | tf_op jit(solution)/shard_map/all_to_all | solution.py:293
  209.5 2.3 %last.1 = bf16[16,256,128]{2,1,0:T(8,128)(2,1)} custom-call(bf16[128,16,256]{2,1,0:T(8,128)(2,1)S(1)} %all_to_all.41.tri_ref, bf16[16,128,256]{2,1,0:T(8,128)(2,1)S(1)} %get-tuple-element.40.z_ref, f32[16,128,256]{2,1,0:T(8,128)S(1)} %get-tuple-element.42.gate_ref, bf16[2,128,128]{2,1,0:T(8,128)(2,1)S(1)} %copy-done.4), custom_call_target="tpu_custom_call" | custom-call | tf_op jit(solution)/shard_map/last/pallas_call | solution.py:276
  (13 shorter events, 0.5 us)
Async XLA Ops:
  0.0 0.9 copy-start
  1.0 1.2 copy-start.2
  73.2 2.7 %collective-permute-start = (bf16[64,2,16,256]{3,2,1,0:T(8,128)(2,1)S(1)}, bf16[64,2,16,256]{3,2,1,0:T(8,128)(2,1)S(1)}, u32[]{:S(2)}, u32[]{:S(2)}) collective-permute-start(bf16[64,2,16,256]{3,2,1,0:T(8,128)(2,1)S(1)} %other.1), channel_id=1, source_target_pairs={{0,1},{1,0},{2,3},{3,2},{4,5},{5,4},{6,7},{7,6},{8,9},{9,8},{10,11... | collective-permute-start | bytes 3145736 | tf_op jit(solution)/shard_map/ppermute | solution.py:138
  76.3 41.1 %copy-start.1 = (bf16[2,128,512]{2,1,0:T(8,128)(2,1)S(1)}, bf16[2,128,512]{2,1,0:T(8,128)(2,1)}, u32[]{:S(2)}) copy-start(bf16[2,128,512]{2,1,0:T(8,128)(2,1)} %w_in_ref.3) | copy-start | bytes 786436
  76.3 41.1 %copy-start.3 = (bf16[2,128,128]{2,1,0:T(8,128)(2,1)S(1)}, bf16[2,128,128]{2,1,0:T(8,128)(2,1)}, u32[]{:S(2)}) copy-start(bf16[2,128,128]{2,1,0:T(8,128)(2,1)} %w_gate_ref.3) | copy-start | bytes 196612
  76.3 41.1 %copy-start.4 = (bf16[2,128,128]{2,1,0:T(8,128)(2,1)S(1)}, bf16[2,128,128]{2,1,0:T(8,128)(2,1)}, u32[]{:S(2)}) copy-start(bf16[2,128,128]{2,1,0:T(8,128)(2,1)} %w_out_ref.3) | copy-start | bytes 196612
  170.0 2.7 %collective-permute-start.1 = (bf16[64,2,16,256]{3,2,1,0:T(8,128)(2,1)S(1)}, bf16[64,2,16,256]{3,2,1,0:T(8,128)(2,1)S(1)}, u32[]{:S(2)}, u32[]{:S(2)}) collective-permute-start(bf16[64,2,16,256]{3,2,1,0:T(8,128)(2,1)S(1)} %slice.20), channel_id=1, source_target_pairs={{0,1},{1,0},{2,3},{3,2},{4,5},{5,4},{6,7},{7,6},{8,9},{9,8},{10,11... | collective-permute-start | bytes 3145736 | tf_op jit(solution)/shard_map/ppermute | solution.py:195

commit v7 on v6

--- a/solution.py
+++ b/solution.py
@@ -327,7 +327,7 @@
     tri = lax.cond(core[0] == 0, at_once, plane_first, *tri)
     sent, z = middle(tri, z, w_gate, w_out, w_in)
     tri, gates = incoming(exchange(sent), core, z, w_gate)
-    return last(exchange(tri), z, gates, w_out)
+    return last(lax.cond(core[0] == 0, exchange, plane_then_z, tri), z, gates, w_out)
 
 
 def solution(mesh):

time: 214 us -> 220 us (1.028)
  Pallas kernels: 13.8 us -> 17.8 us
  blocking collectives: 191 us -> 194 us
    all_to_all x4 -> x6, blocking collectives: 108 us -> 146 us  [along(): lax.all_to_all(blocks, axes, split_axis=0, concat_axis=0, tiled=True)]
    all_to_all x2 -> x1, blocking collectives: 83.5 us -> 47.6 us  [exchange(): lax.all_to_all(blocks, CHIPS, split_axis=0, concat_axis=0, tiled=True)]
where the time goes in v7:
time: 220 us; the launch traced here: 219 us
  blocking collectives  194 us (88%)
  Pallas kernels  17.8 us (8%)
  local copies, waits for them, and re-layouts  4.16 us (2%)
  waiting for transfers between devices  2.99 us (1%)
    all_to_all x6, blocking collectives, along(): lax.all_to_all(blocks, axes, split_axis=0, concat_axis=0, tiled=True)  146 us
    all_to_all x1, blocking collectives, exchange(): lax.all_to_all(blocks, CHIPS, split_axis=0, concat_axis=0, tiled=True)  47.6 us
    pallas_call x1, Pallas kernels, middle(): pl.pallas_call(middle_kernel, out_shape=(jax.ShapeDtypeStruct((hidden, 2...  5.95 us
  transfers between devices with their start and end apart: 2, of which 2 were waited for; matrix products, arithmetic and copies ran while one was open for 0% of the time, Pallas kernels for 1%

profile of v7, /device:TPU:1, one launch (start us, length us, event | category | flops | bytes accessed | tf_op | source)
XLA Modules:
  0.0 219.4 jit_solution(938697092025807653)
XLA Ops:
  0.0 0.9 copy-done
  1.0 1.2 copy-done.2
  2.2 2.6 %first.1 = (bf16[128,32,256]{2,1,0:T(8,128)(2,1)S(1)}, bf16[16,128,256]{2,1,0:T(8,128)(2,1)S(1)}) custom-call(s32[1]{0:T(128)} %bitcast.17.core_ref, bf16[16,256,128]{2,1,0:T(8,128)(2,1)S(1)} %copy-done.2, bf16[2,128,512]{2,1,0:T(8,128)(2,1)S(1)} %copy-done), custom_call_target="tpu_custom_call" | custom-call | tf_op jit(solution)/shard_map/first/pallas_call | solution.py:79
  4.7 67.8 %conditional.3 = (bf16[64,2,32,256]{3,2,1,0:T(8,128)(2,1)}) conditional(s32[]{:T(128)} %convert_element_type.2, bf16[128,32,256]{2,1,0:T(8,128)(2,1)S(1)} %get-tuple-element.39, bf16[128,32,256]{2,1,0:T(8,128)(2,1)S(1)} %get-tuple-element.39), branch_computations={%region_0.0_spmd, %region_1.0_spmd} | conditional | bytes 16777224 | solution.py:326
  4.8 0.2 copy.5
  5.0 27.7 %all_to_all.41 = bf16[16,8,32,256]{3,2,1,0:T(8,128)(2,1)S(1)} all-to-all(bf16[16,8,32,256]{3,2,1,0:T(8,128)(2,1)S(1)} %copy.5), channel_id=1, replica_groups=mesh['z'=8,'x'=4,'yl'=2,'yh'=2,'core'=2] {'x','yl','yh'}, dimensions={0} | all-to-all | bytes 4194304 | tf_op jit(solution)/shard_map/cond/branch_0_fun/all_to_all | solution.py:304
  32.9 39.7 %all_to_all.42 = bf16[8,16,32,256]{3,2,1,0:T(8,128)(2,1)} all-to-all(bf16[8,16,32,256]{3,2,1,0:T(8,128)(2,1)S(1)} %bitcast.35), channel_id=1, replica_groups=mesh['z'=8,'x'=4,'yl'=2,'yh'=2,'core'=2] {'z'}, dimensions={0} | all-to-all | bytes 4194304 | tf_op jit(solution)/shard_map/cond/branch_0_fun/all_to_all | solution.py:301
  72.6 2.5 %other.1 = bf16[64,2,16,256]{3,2,1,0:T(8,128)(2,1)S(1)} custom-call(s32[1]{0:T(128)} %bitcast.17.core_ref, bf16[64,2,32,256]{3,2,1,0:T(8,128)(2,1)} %get-tuple-element.57.got_ref), custom_call_target="tpu_custom_call" | custom-call | tf_op jit(solution)/shard_map/other/pallas_call | solution.py:130
  75.2 0.7 own.1.own_ref
  75.9 1.9 collective-permute-done.other_ref
  77.8 0.3 sum.1
  78.1 41.6 %conditional.4 = (bf16[128,16,128]{2,1,0:T(8,128)(2,1)}, bf16[128,16,128]{2,1,0:T(8,128)(2,1)S(1)}) conditional(s32[]{:T(128)} %convert_element_type.2, (bf16[128,16,128]{2,1,0:T(8,128)(2,1)S(1)}, bf16[128,16,128]{2,1,0:T(8,128)(2,1)S(1)}) %tuple.38, (bf16[128,16,128]{2,1,0:T(8,128)(2,1)S(1)}, bf16[128,16,128]{2,1,0:T(8,128)(2,1)S(1)}) %tuple.39), branch_computations={%region_2.0_spmd, %region_3.0_spmd} | conditional | flops 2097152 | bytes 12582928 | solution.py:327
  78.4 20.1 %all_to_all.44 = bf16[16,8,16,256]{3,2,1,0:T(8,128)(2,1)S(1)} all-to-all(bf16[16,8,16,256]{3,2,1,0:T(8,128)(2,1)S(1)} %copy.7), channel_id=1, replica_groups=mesh['z'=8,'x'=4,'yl'=2,'yh'=2,'core'=2] {'x','yl','yh'}, dimensions={0} | all-to-all | bytes 2097152 | tf_op jit(solution)/shard_map/cond/branch_0_fun/all_to_all | solution.py:304
  98.6 20.2 %all_to_all.45 = bf16[8,16,16,256]{3,2,1,0:T(8,128)(2,1)S(1)} all-to-all(bf16[8,16,16,256]{3,2,1,0:T(8,128)(2,1)S(1)} %bitcast.37), channel_id=1, replica_groups=mesh['z'=8,'x'=4,'yl'=2,'yh'=2,'core'=2] {'z'}, dimensions={0} | all-to-all | bytes 2097152 | tf_op jit(solution)/shard_map/cond/branch_0_fun/all_to_all | solution.py:301
  118.8 1.0 fusion
  119.8 6.0 %middle.1 = (bf16[128,32,256]{2,1,0:T(8,128)(2,1)S(1)}, bf16[16,128,256]{2,1,0:T(8,128)(2,1)S(1)}) custom-call(bf16[128,16,128]{2,1,0:T(8,128)(2,1)} %get-tuple-element.42.a_ref, bf16[128,16,128]{2,1,0:T(8,128)(2,1)S(1)} %get-tuple-element.43.b_ref, bf16[16,128,256]{2,1,0:T(8,128)(2,1)S(1)} %get-tuple-element.44.z_ref, bf16[2,128,128]{2,1,0:T(8,128)(2,1)S(1)} %copy-done.3, ...), custom_call_target="tpu_custom_call" | custom-call | tf_op jit(solution)/shard_map/middle/pallas_call | solution.py:242
  125.7 47.6 %all_to_all.50 = bf16[128,32,256]{2,1,0:T(8,128)(2,1)S(1)} all-to-all(bf16[128,32,256]{2,1,0:T(8,128)(2,1)S(1)} %get-tuple-element.45), channel_id=1, replica_groups=mesh['z'=8,'x'=4,'yl'=2,'yh'=2,'core'=2] {'z','x','yl','yh'}, dimensions={0} | all-to-all | bytes 4194304 | tf_op jit(solution)/shard_map/all_to_all | solution.py:293
  173.6 1.5 near.1
  175.1 1.1 collective-permute-done.1.left_ref
  176.2 0.8 far.1
  177.0 38.7 %conditional.5 = (bf16[128,16,256]{2,1,0:T(8,128)(2,1)}) conditional(s32[]{:T(128)} %convert_element_type.2, bf16[64,2,16,256]{3,2,1,0:T(8,128)(2,1)S(1)} %far.1, bf16[64,2,16,256]{3,2,1,0:T(8,128)(2,1)S(1)} %far.1), branch_computations={%region_4.0_spmd, %region_5.0_spmd} | conditional | bytes 8388616 | solution.py:330
  177.1 17.6 %all_to_all.47 = bf16[16,8,16,256]{3,2,1,0:T(8,128)(2,1)S(1)} all-to-all(bf16[16,8,16,256]{3,2,1,0:T(8,128)(2,1)S(1)} %copy.9), channel_id=1, replica_groups=mesh['z'=8,'x'=4,'yl'=2,'yh'=2,'core'=2] {'x','yl','yh'}, dimensions={0} | all-to-all | bytes 2097152 | tf_op jit(solution)/shard_map/cond/branch_0_fun/all_to_all | solution.py:304
  194.8 20.9 %all_to_all.48 = bf16[8,16,16,256]{3,2,1,0:T(8,128)(2,1)} all-to-all(bf16[8,16,16,256]{3,2,1,0:T(8,128)(2,1)S(1)} %bitcast.38), channel_id=1, replica_groups=mesh['z'=8,'x'=4,'yl'=2,'yh'=2,'core'=2] {'z'}, dimensions={0} | all-to-all | bytes 2097152 | tf_op jit(solution)/shard_map/cond/branch_0_fun/all_to_all | solution.py:301
  215.7 3.5 %last.1 = bf16[16,256,128]{2,1,0:T(8,128)(2,1)} custom-call(bf16[128,16,256]{2,1,0:T(8,128)(2,1)} %get-tuple-element.58.tri_ref, bf16[16,128,256]{2,1,0:T(8,128)(2,1)S(1)} %get-tuple-element.46.z_ref, f32[16,128,256]{2,1,0:T(8,128)S(1)} %get-tuple-element.48.gate_ref, bf16[2,128,128]{2,1,0:T(8,128)(2,1)S(1)} %copy-done.4), custom_call_target="tpu_custom_call" | custom-call | tf_op jit(solution)/shard_map/last/pallas_call | solution.py:276
  (19 shorter events, 1.1 us)
Async XLA Ops:
  0.0 0.9 copy-start
  1.0 1.2 copy-start.2
  72.6 2.6 %copy-start.5 = (bf16[64,2,32,256]{3,2,1,0:T(8,128)(2,1)S(1)}, bf16[64,2,32,256]{3,2,1,0:T(8,128)(2,1)}, u32[]{:S(2)}) copy-start(bf16[64,2,32,256]{3,2,1,0:T(8,128)(2,1)} %get-tuple-element.57.got_ref) | copy-start | bytes 6291460
  75.1 2.7 %collective-permute-start = (bf16[64,2,16,256]{3,2,1,0:T(8,128)(2,1)S(1)}, bf16[64,2,16,256]{3,2,1,0:T(8,128)(2,1)S(1)}, u32[]{:S(2)}, u32[]{:S(2)}) collective-permute-start(bf16[64,2,16,256]{3,2,1,0:T(8,128)(2,1)S(1)} %other.1), channel_id=1, source_target_pairs={{0,1},{1,0},{2,3},{3,2},{4,5},{5,4},{6,7},{7,6},{8,9},{9,8},{10,11... | collective-permute-start | bytes 3145736 | tf_op jit(solution)/shard_map/ppermute | solution.py:138
  78.1 41.7 %copy-start.1 = (bf16[2,128,512]{2,1,0:T(8,128)(2,1)S(1)}, bf16[2,128,512]{2,1,0:T(8,128)(2,1)}, u32[]{:S(2)}) copy-start(bf16[2,128,512]{2,1,0:T(8,128)(2,1)} %w_in_ref.3) | copy-start | bytes 786436
  78.1 41.6 %copy-start.3 = (bf16[2,128,128]{2,1,0:T(8,128)(2,1)S(1)}, bf16[2,128,128]{2,1,0:T(8,128)(2,1)}, u32[]{:S(2)}) copy-start(bf16[2,128,128]{2,1,0:T(8,128)(2,1)} %w_gate_ref.3) | copy-start | bytes 196612
  78.1 41.6 %copy-start.4 = (bf16[2,128,128]{2,1,0:T(8,128)(2,1)S(1)}, bf16[2,128,128]{2,1,0:T(8,128)(2,1)}, u32[]{:S(2)}) copy-start(bf16[2,128,128]{2,1,0:T(8,128)(2,1)} %w_out_ref.3) | copy-start | bytes 196612
  173.5 2.7 %collective-permute-start.1 = (bf16[64,2,16,256]{3,2,1,0:T(8,128)(2,1)S(1)}, bf16[64,2,16,256]{3,2,1,0:T(8,128)(2,1)S(1)}, u32[]{:S(2)}, u32[]{:S(2)}) collective-permute-start(bf16[64,2,16,256]{3,2,1,0:T(8,128)(2,1)S(1)} %slice.20), channel_id=1, source_target_pairs={{0,1},{1,0},{2,3},{3,2},{4,5},{5,4},{6,7},{7,6},{8,9},{9,8},{10,11... | collective-permute-start | bytes 3145736 | tf_op jit(solution)/shard_map/ppermute | solution.py:195
